TPU v7x, 1024 devices: a whole 4x4x32 slice. The times are simulated.
1024 devices in a mesh: curve: 256 (over y, z, core), group: 4 (over x).
Axes of the slice: x: 4, y: 4, z: 32, core: 2. Of those that a mesh axis runs over, the one named last changes fastest.
Arguments:
- tangent: float32 [5, 64, 131072], P(None, None, ('curve', 'group')), may hold values from -6 to 6
- flux_jacobian: float32 [3, 5, 5, 131072], P(None, None, None, ('curve', 'group')), may hold values from -1.75 to 1.75
- viscosity: float32 [131072], P(('curve', 'group')), may hold values from 0.02 to 0.2
- neighbours: int32 [6, 131072], P(None, ('curve', 'group')), may hold values from -2 to 131071, as said below
- send_table: int32 [3, 131072], P(None, ('curve', 'group')), may hold values from 0 to 127, as said below
- recv_table: int32 [4, 131072], P(None, ('curve', 'group')), may hold values from 0 to 127, as said below
Outputs:
- first_image: float32 [5, 64, 131072], P(None, None, ('curve', 'group'))
- second_image: float32 [5, 64, 131072], P(None, None, ('curve', 'group'))
Inputs may be any that keep to these rules, and one draw needn't show every extreme that they name: `neighbours`: each entry is -1 (wall), -2 (a fine or coarse face of a mortar slot in use), or the id of the element across the face. Ids are Morton positions; device d holds ids d * 128 to (d + 1) * 128 - 1, and a neighbour id lies at most 64 ids before or after its element's device range; that distance is reached. Across an even face the neighbour id is lower than the element's, across an odd face higher. The neighbour's matching face is f xor 1, with face nodes in the same order. `send_table`: each device's 4 * 32 slots are grouped by destination index in its group, 32 slots each, used slots first. Row 0: local index of the fine element, row 1: its face, row 2: 1 if used, else 0; unused slots hold zeros. A device names each of its (element, face) pairs at most once. In every group one device receives exactly 32 used slots from every device of the group. `recv_table`: each device's slots are grouped by source index in its group, in the sender's slot order. Row 0: local index of the coarse element, row 1: its face, the fine face xor 1, row 2: the child position 0 to 3, row 3: the sender's used flag; unused slots hold zeros.
All inputs are finite; a program needn't handle non-finite values.
Results may differ from a plain program's by a relative error of at most 0.0001.
Values sent between devices are 32-bit elements; how exact they have to be, the bound alone decides.
No kernel may reach another device: no remote copies, remote signals or barrier semaphores. Data moves between devices by JAX's collectives and lax.ppermute only.
A program may use at most 128 MiB of HBM per device.

v0:
```python
import functools

import jax
import jax.numpy as jnp
import ml_dtypes
import numpy as np
from jax import lax
from jax.experimental import pallas as pl
from jax.experimental.pallas import tpu as pltpu
from jax.sharding import PartitionSpec as P

F32 = jnp.float32
BF16 = jnp.bfloat16
AXES = ("curve", "group")
PSEUDO_STEP = 0.05
FACE_SCALE = 0.15


def node_tables():
    points = np.array([-1.0, -1.0 / np.sqrt(5.0), 1.0 / np.sqrt(5.0), 1.0])
    weights = np.array([1.0, 5.0, 5.0, 1.0]) / 6.0
    barycentric = np.array(
        [1.0 / np.prod([points[j] - points[k] for k in range(4) if k != j]) for j in range(4)]
    )
    derivative = np.zeros((4, 4))
    for a in range(4):
        for b in range(4):
            if a != b:
                derivative[a, b] = barycentric[b] / barycentric[a] / (points[a] - points[b])
        derivative[a, a] = -np.sum(derivative[a])
    halves = []
    for upper_half in range(2):
        matrix = np.zeros((4, 4))
        for a in range(4):
            target = 0.5 * points[a] + upper_half - 0.5
            for b in range(4):
                matrix[a, b] = np.prod(
                    [(target - points[k]) / (points[b] - points[k]) for k in range(4) if k != b]
                )
        halves.append(matrix)
    surface_weights = np.kron(weights, weights)
    interpolate = np.stack([np.kron(halves[c // 2], halves[c % 2]) for c in range(4)])
    project = np.stack(
        [
            0.25 * (interpolate[c].T * surface_weights[None, :]) / surface_weights[:, None]
            for c in range(4)
        ]
    )
    return derivative, interpolate, project


def pieces_of(matrix):
    hi = matrix.astype(ml_dtypes.bfloat16)
    lo = (matrix - hi.astype(np.float64)).astype(ml_dtypes.bfloat16)
    return np.concatenate([hi, hi, lo], axis=1)


def operator_tables():
    derivative, interpolate, project = node_tables()
    eye = np.eye(4)
    d_x = np.kron(eye, np.kron(eye, derivative))
    d_y = np.kron(eye, np.kron(derivative, eye))
    d_z = np.kron(derivative, np.kron(eye, eye))
    laplacian = d_x @ d_x + d_y @ d_y + d_z @ d_z
    volume = pieces_of(np.concatenate([d_x, d_y, d_z, laplacian], axis=0))
    return (
        volume,
        pieces_of(interpolate.reshape(64, 16)),
        pieces_of(project.reshape(64, 16)),
    )


def split(x):
    hi = x.astype(BF16)
    lo = (x - hi.astype(F32)).astype(BF16)
    return hi, lo


def dot(a, b):
    return lax.dot_general(a, b, (((1,), (0,)), ((), ())), preferred_element_type=F32)


def one_hot(index, rows):
    place = lax.broadcasted_iota(jnp.int32, (rows, index.shape[1]), 0)
    return jnp.where(place == index, 1.0, 0.0).astype(BF16)


def slot_one_hots(send_ref, recv_ref):
    fine = jnp.where(send_ref[2:3, :] > 0, send_ref[1:2, :] * 128 + send_ref[0:1, :], -1)
    coarse = jnp.where(recv_ref[3:4, :] > 0, recv_ref[1:2, :] * 128 + recv_ref[0:1, :], -1)
    return jnp.concatenate([one_hot(fine, 768), one_hot(coarse, 768)], axis=1)


def by_child(table_ref, values, recv_ref):
    count = len(values)
    hi, lo = split(jnp.concatenate(values, axis=1))
    product = dot(table_ref[...], jnp.concatenate([hi, lo, hi], axis=0))
    child = recv_ref[2:3, :]
    picks = [jnp.where(child == c, 1.0, 0.0) for c in range(4)]
    return [
        sum(
            product[16 * c : 16 * c + 16, 128 * n : 128 * n + 128] * picks[c]
            for c in range(4)
        )
        for n in range(count)
    ]


def face_values(v_ref, face, a):
    d, s = face // 2, face % 2
    if d == 0:
        return v_ref[a, pl.ds(3 * s, 16, stride=4), :]
    if d == 1:
        return jnp.concatenate(
            [v_ref[a, 16 * k + 12 * s : 16 * k + 12 * s + 4, :] for k in range(4)], axis=0
        )
    return v_ref[a, 48 * s : 48 * s + 16, :]


def add_to_face(o_ref, face, a, values):
    d, s = face // 2, face % 2
    if d == 0:
        o_ref[a, pl.ds(3 * s, 16, stride=4), :] += values
    elif d == 1:
        for k in range(4):
            row = 16 * k + 12 * s
            o_ref[a, row : row + 4, :] += values[4 * k : 4 * k + 4]
    else:
        o_ref[a, 48 * s : 48 * s + 16, :] += values


def trace_part(v_ref, j_ref, send_ref, recv_ref, it_ref, g_ref, loc_ref, up_ref, down_ref, m_ref):
    gs, hs = [], []
    for f in range(6):
        normal = 2.0 * (f % 2) - 1.0
        w = [face_values(v_ref, f, b) for b in range(5)]
        g_rows, h_rows = [], []
        for a in range(5):
            q = j_ref[f // 2, a, 0:1, :] * w[0]
            for b in range(1, 5):
                q = q + j_ref[f // 2, a, b : b + 1, :] * w[b]
            q = normal * q
            g_rows.append(w[a] + q)
            h_rows.append(w[a] - q)
        gs.append(jnp.concatenate(g_rows, axis=0))
        hs.append(jnp.concatenate(h_rows, axis=0))
        g_ref[f] = gs[f]
    lane = lax.broadcasted_iota(jnp.int32, (120, 128), 1)
    odd = jnp.concatenate([gs[1], gs[3], gs[5]], axis=0)
    even = jnp.concatenate([gs[0], gs[2], gs[4]], axis=0)
    up_ref[...] = jnp.where(lane < 64, pltpu.roll(odd[:120], 64, 1), odd[120:])
    down_ref[...] = jnp.where(lane < 64, even[:120], pltpu.roll(even[120:], 64, 1))
    hots = slot_one_hots(send_ref, recv_ref)
    g_hi, g_lo = split(jnp.concatenate(gs, axis=1))
    h_hi, h_lo = split(jnp.concatenate(hs, axis=1))
    picked = dot(jnp.concatenate([g_hi, g_lo, h_hi, h_lo], axis=0), hots)
    g_slots = picked[0:80] + picked[80:160]
    h_slots = picked[160:240] + picked[240:320]
    g_fine, g_coarse = g_slots[:, :128], g_slots[:, 128:]
    h_fine, h_coarse = h_slots[:, :128], h_slots[:, 128:]
    rows = [g_coarse[16 * a : 16 * a + 16] for a in range(5)]
    rows += [h_coarse[16 * a : 16 * a + 16] for a in range(5)]
    inter = by_child(it_ref, rows, recv_ref)
    g_inter = jnp.concatenate(inter[:5], axis=0)
    h_inter = jnp.concatenate(inter[5:], axis=0)
    loc_ref[...] = jnp.concatenate([h_inter, h_fine], axis=0)
    outgoing = jnp.concatenate([g_fine, g_inter], axis=0)
    quarter = lax.broadcasted_iota(jnp.int32, (40, 128), 1) // 32
    for t in range(4):
        block = None
        for q in range(4):
            part = outgoing[40 * q : 40 * q + 40]
            shift = (32 * (q - t)) % 128
            part = pltpu.roll(part, shift, 1) if shift else part
            block = part if block is None else jnp.where(quarter == q, part, block)
        m_ref[t] = block


def combine_part(
    base_ref, g_ref, loc_ref, before_ref, after_ref, m_ref, nb_ref, send_ref, recv_ref, pt_ref, o_ref
):
    first_id = (lax.axis_index("curve") * 4 + lax.axis_index("group")) * 128
    o_ref[...] = base_ref[...]
    quarter = lax.broadcasted_iota(jnp.int32, (40, 128), 1) // 32
    parts = []
    for q in range(4):
        part = None
        for s in range(4):
            shift = (32 * (s - q)) % 128
            block = m_ref[s]
            block = pltpu.roll(block, shift, 1) if shift else block
            part = block if part is None else jnp.where(quarter == s, block, part)
        parts.append(part)
    incoming = jnp.concatenate(parts, axis=0) - loc_ref[...]
    projected = by_child(pt_ref, [incoming[16 * a : 16 * a + 16] for a in range(5)], recv_ref)
    values = jnp.concatenate([incoming[80:160], jnp.concatenate(projected, axis=0)], axis=1)
    hi, lo = split(values)
    hots = slot_one_hots(send_ref, recv_ref)
    spread = lax.dot_general(
        jnp.concatenate([hi, lo], axis=0),
        hots,
        (((1,), (1,)), ((), ())),
        preferred_element_type=F32,
    )
    mortar = spread[0:80] + spread[80:160]
    before, after = before_ref[...], after_ref[...]
    before = jnp.concatenate([before, pltpu.roll(before, 64, 1)], axis=0)
    after = jnp.concatenate([after, pltpu.roll(after, 64, 1)], axis=0)
    for f in range(6):
        linked = nb_ref[f : f + 1, :]
        place = linked - first_id
        if f % 2 == 0:
            halo = before
            place = jnp.where(place < 0, place + 192, place)
        else:
            halo = after
        place = jnp.where(linked < 0, -1, place)
        third = f // 2
        source = jnp.concatenate([g_ref[f ^ 1], halo[80 * third : 80 * third + 80]], axis=1)
        hi, lo = split(source)
        far = dot(jnp.concatenate([hi, lo], axis=0), one_hot(place, 256))
        total = far[0:80] + far[80:160] + mortar[:, 128 * f : 128 * f + 128]
        total = total * (-FACE_SCALE)
        for a in range(5):
            add_to_face(o_ref, f, a, total[16 * a : 16 * a + 16])


def trace_kernel(v_ref, j_ref, send_ref, recv_ref, it_ref, g_ref, loc_ref, up_ref, down_ref, m_ref):
    trace_part(v_ref, j_ref, send_ref, recv_ref, it_ref, g_ref, loc_ref, up_ref, down_ref, m_ref)


def volume_kernel(v_ref, j_ref, visc_ref, nb_ref, g_ref, vt_ref, o_ref):
    v = v_ref[...]
    hi, lo = split(jnp.concatenate([v[a] for a in range(5)], axis=1))
    terms = dot(vt_ref[...], jnp.concatenate([hi, lo, hi], axis=0))
    visc = visc_ref[...].reshape(1, 128)
    for a in range(5):
        total = visc * terms[192:256, 128 * a : 128 * a + 128]
        for d in range(3):
            for b in range(5):
                total = total - j_ref[d, a, b : b + 1, :] * terms[
                    64 * d : 64 * d + 64, 128 * b : 128 * b + 128
                ]
        o_ref[a] = v[a] - PSEUDO_STEP * total
    for f in range(6):
        mask = jnp.where(nb_ref[f : f + 1, :] != -2, FACE_SCALE, 0.0)
        for a in range(5):
            h = 2.0 * face_values(v_ref, f, a) - g_ref[f, 16 * a : 16 * a + 16, :]
            add_to_face(o_ref, f, a, mask * h)


def middle_kernel(
    base_ref, g_ref, loc_ref, before_ref, after_ref, m_ref, nb_ref, send_ref, recv_ref,
    j_ref, it_ref, pt_ref,
    o_ref, g2_ref, loc2_ref, up_ref, down_ref, m2_ref,
):
    combine_part(
        base_ref, g_ref, loc_ref, before_ref, after_ref, m_ref, nb_ref, send_ref, recv_ref, pt_ref, o_ref
    )
    trace_part(o_ref, j_ref, send_ref, recv_ref, it_ref, g2_ref, loc2_ref, up_ref, down_ref, m2_ref)


def final_kernel(
    base_ref, g_ref, loc_ref, before_ref, after_ref, m_ref, nb_ref, send_ref, recv_ref, pt_ref, o_ref
):
    combine_part(
        base_ref, g_ref, loc_ref, before_ref, after_ref, m_ref, nb_ref, send_ref, recv_ref, pt_ref, o_ref
    )


def shape(*dims):
    return jax.ShapeDtypeStruct(dims, F32)


def call(kernel, outs, *args):
    return pl.pallas_call(
        kernel,
        out_shape=outs,
        compiler_params=pltpu.CompilerParams(vmem_limit_bytes=32 * 1024 * 1024),
    )(*args)


IMAGE = (5, 64, 128)
TRACES = (shape(6, 80, 128), shape(160, 128), shape(120, 128), shape(120, 128), shape(4, 40, 128))


def exchange(up, down, mortar):
    count = lax.axis_size(AXES)
    onward = [(i, i + 1) for i in range(count - 1)]
    back = [(i + 1, i) for i in range(count - 1)]
    mortar = lax.all_to_all(mortar, "group", split_axis=0, concat_axis=0, tiled=True)
    before = lax.ppermute(up, AXES, onward)
    after = lax.ppermute(down, AXES, back)
    return before, after, mortar


def local(tangent, jacobian, viscosity, neighbours, send_table, recv_table):
    volume_table, inter_table, project_table = (jnp.asarray(t) for t in operator_tables())
    g, loc, up, down, mortar = call(
        trace_kernel, TRACES, tangent, jacobian, send_table, recv_table, inter_table
    )
    before, after, mortar = exchange(up, down, mortar)
    base = call(
        volume_kernel, shape(*IMAGE), tangent, jacobian, viscosity, neighbours, g, volume_table
    )
    first, g, loc, up, down, mortar = call(
        middle_kernel,
        (shape(*IMAGE),) + TRACES,
        base, g, loc, before, after, mortar, neighbours, send_table, recv_table,
        jacobian, inter_table, project_table,
    )
    before, after, mortar = exchange(up, down, mortar)
    base = call(
        volume_kernel, shape(*IMAGE), first, jacobian, viscosity, neighbours, g, volume_table
    )
    second = call(
        final_kernel,
        shape(*IMAGE),
        base, g, loc, before, after, mortar, neighbours, send_table, recv_table, project_table,
    )
    return first, second


def solution(mesh):
    in_specs = (
        P(None, None, AXES),
        P(None, None, None, AXES),
        P(AXES),
        P(None, AXES),
        P(None, AXES),
        P(None, AXES),
    )
    out_specs = (P(None, None, AXES), P(None, None, AXES))
    return jax.shard_map(local, mesh=mesh, in_specs=in_specs, out_specs=out_specs, check_vma=False)
```

profile of v0, /device:TPU:24, one launch (start us, length us, event | category | flops | bytes accessed | tf_op | source)
XLA Modules:
  0.0 51.3 jit_solution(12545925039108953623)
XLA Ops:
  0.6 0.0 copy-start.6
  0.6 0.0 copy-start.8
  0.7 0.0 copy-start.7
  0.7 0.8 %copy.12.j_ref = f32[3,5,5,128]{3,2,1,0:T(8,128)S(1)} copy(f32[3,5,5,128]{3,0,2,1:T(4,128)} %param.10) | data formatting | bytes 76800 | tf_op args[1]
  1.5 0.0 copy-done.6
  1.5 0.0 copy-done.8
  1.5 0.0 copy-done.7
  1.5 0.0 copy-start
  1.5 0.9 %copy-done = f32[5,64,128]{2,1,0:T(8,128)S(1)} copy-done((f32[5,64,128]{2,1,0:T(8,128)S(1)}, f32[5,64,128]{2,1,0:T(8,128)}, u32[]{:S(2)}) %copy-start) | copy-done | bytes 163864
  2.4 0.0 copy-start.1
  2.4 1.2 %shard_map.104 = (f32[6,80,128]{2,1,0:T(8,128)S(1)}, f32[160,128]{1,0:T(8,128)S(1)}, f32[120,128]{1,0:T(8,128)S(1)}, f32[120,128]{1,0:T(8,128)S(1)}, f32[4,40,128]{2,1,0:T(8,128)}) custom-call(f32[5,64,128]{2,1,0:T(8,128)S(1)} %copy-done, f32[3,5,5,128]{3,2,1,0:T(8,128)S(1)} %copy.12.j_ref, s32[3,128]{1,0:T(4,128)S(1)} %copy-done.7, s32[4,128]{1,0:T(4,128)S(1)} %copy-done.8, ...), custom_call_target="tpu_custom_call" | custom-call | tf_op jit(solution)/shard_map/pallas_call | solution.py:276
  3.6 0.0 copy-start.2
  3.6 4.4 %all-to-all-start = ((f32[4,40,128]{2,1,0:T(8,128)}), f32[4,40,128]{2,1,0:T(8,128)S(1)}, u32[]{:S(2)}, u32[]{:S(2)}) async-start(f32[4,40,128]{2,1,0:T(8,128)} %get-tuple-element.17), calls=%async_computation | async-start | bytes 163840 | tf_op jit(solution)/shard_map/all_to_all | solution.py:291
  8.1 0.0 copy-start.4
  8.1 4.1 %collective-permute-start = (f32[120,128]{1,0:T(8,128)S(1)}, f32[120,128]{1,0:T(8,128)S(1)}, u32[]{:S(2)}, u32[]{:S(2)}) collective-permute-start(f32[120,128]{1,0:T(8,128)S(1)} %get-tuple-element.15), channel_id=1, source_target_pairs={{0,1},{1,2},{2,3},{3,4},{4,5},{5,6},{6,7},{7,8},{8,9},{9,10},{10,1... | collective-permute-start | bytes 184328 | tf_op jit(solution)/shard_map/ppermute | solution.py:292
  12.1 0.0 copy-start.9
  12.1 18.4 %collective-permute-start.1 = (f32[120,128]{1,0:T(8,128)S(1)}, f32[120,128]{1,0:T(8,128)S(1)}, u32[]{:S(2)}, u32[]{:S(2)}) collective-permute-start(f32[120,128]{1,0:T(8,128)S(1)} %get-tuple-element.16), channel_id=1, source_target_pairs={{1,0},{2,1},{3,2},{4,3},{5,4},{6,5},{7,6},{8,7},{9,8},{10,9},{11,1... | collective-permute-start | bytes 184328 | tf_op jit(solution)/shard_map/ppermute | solution.py:293
  30.5 0.0 copy-done.1
  30.6 0.0 copy-done.2
  30.6 0.0 copy-done.4
  30.6 0.0 copy-done.9
  30.6 0.0 copy-start.5
  30.6 0.5 shard_map.105.base_ref
  31.1 0.0 all-to-all-done.m_ref
  31.1 0.0 collective-permute-done.before_ref
  31.1 1.3 %collective-permute-done.1.after_ref = f32[120,128]{1,0:T(8,128)S(1)} collective-permute-done((f32[120,128]{1,0:T(8,128)S(1)}, f32[120,128]{1,0:T(8,128)S(1)}, u32[]{:S(2)}, u32[]{:S(2)}) %collective-permute-start.1) | collective-permute-done | bytes 61472 | tf_op jit(solution)/shard_map/ppermute | solution.py:293
  32.4 0.0 copy-done.5
  32.4 1.9 %shard_map.106 = (f32[5,64,128]{2,1,0:T(8,128)}, f32[6,80,128]{2,1,0:T(8,128)S(1)}, f32[160,128]{1,0:T(8,128)S(1)}, f32[120,128]{1,0:T(8,128)S(1)}, f32[120,128]{1,0:T(8,128)S(1)}, /*index=5*/f32[4,40,128]{2,1,0:T(8,128)}) custom-call(f32[5,64,128]{2,1,0:T(8,128)S(1)} %shard_map.105.base_ref, f32[6,80,128]{2,1,0:T(8,128)S(1)} %get-tuple-element.13.g_ref, ...), custom_call_target="tpu_custom_call" | custom-call | tf_op jit(solution)/shard_map/pallas_call | solution.py:276
  34.3 0.0 copy-start.3
  34.3 3.4 %all-to-all-start.1 = ((f32[4,40,128]{2,1,0:T(8,128)}), f32[4,40,128]{2,1,0:T(8,128)S(1)}, u32[]{:S(2)}, u32[]{:S(2)}) async-start(f32[4,40,128]{2,1,0:T(8,128)} %get-tuple-element.23), calls=%async_computation.1 | async-start | bytes 163840 | tf_op jit(solution)/shard_map/all_to_all | solution.py:291
  37.7 3.9 %collective-permute-start.2 = (f32[120,128]{1,0:T(8,128)S(1)}, f32[120,128]{1,0:T(8,128)S(1)}, u32[]{:S(2)}, u32[]{:S(2)}) collective-permute-start(f32[120,128]{1,0:T(8,128)S(1)} %get-tuple-element.21), channel_id=1, source_target_pairs={{0,1},{1,2},{2,3},{3,4},{4,5},{5,6},{6,7},{7,8},{8,9},{9,10},{10,1... | collective-permute-start | bytes 184328 | tf_op jit(solution)/shard_map/ppermute | solution.py:292
  41.6 6.6 %collective-permute-start.3 = (f32[120,128]{1,0:T(8,128)S(1)}, f32[120,128]{1,0:T(8,128)S(1)}, u32[]{:S(2)}, u32[]{:S(2)}) collective-permute-start(f32[120,128]{1,0:T(8,128)S(1)} %get-tuple-element.22), channel_id=1, source_target_pairs={{1,0},{2,1},{3,2},{4,3},{5,4},{6,5},{7,6},{8,7},{9,8},{10,9},{11,1... | collective-permute-start | bytes 184328 | tf_op jit(solution)/shard_map/ppermute | solution.py:293
  48.2 0.0 copy-done.3
  48.2 0.5 shard_map.107.base_ref
  48.7 0.0 all-to-all-done.1.m_ref
  48.7 0.0 collective-permute-done.2.before_ref
  48.7 1.3 %collective-permute-done.3.after_ref = f32[120,128]{1,0:T(8,128)S(1)} collective-permute-done((f32[120,128]{1,0:T(8,128)S(1)}, f32[120,128]{1,0:T(8,128)S(1)}, u32[]{:S(2)}, u32[]{:S(2)}) %collective-permute-start.3) | collective-permute-done | bytes 61472 | tf_op jit(solution)/shard_map/ppermute | solution.py:293
  50.1 1.3 %shard_map.108 = f32[5,64,128]{2,1,0:T(8,128)} custom-call(f32[5,64,128]{2,1,0:T(8,128)S(1)} %shard_map.107.base_ref, f32[6,80,128]{2,1,0:T(8,128)S(1)} %get-tuple-element.19.g_ref, f32[160,128]{1,0:T(8,128)S(1)} %get-tuple-element.20.loc_ref, f32[120,128]{1,0:T(8,128)S(1)} %collective-permute-done.2.before_ref, ...), custom_call_target="tpu_custom_call" | custom-call | tf_op jit(solution)/shard_map/pallas_call | solution.py:276
Async XLA Ops:
  0.6 0.9 %copy-start.6 = (bf16[64,48]{1,0:T(8,128)(2,1)S(1)}, bf16[64,48]{1,0:T(8,128)(2,1)}, u32[]{:S(2)}) copy-start(bf16[64,48]{1,0:T(8,128)(2,1)} %constant.7.clone.it_ref) | copy-start | bytes 18436
  0.6 0.9 %copy-start.8 = (s32[4,128]{1,0:T(4,128)S(1)}, s32[4,128]{1,0:T(4,128)}, u32[]{:S(2)}) copy-start(s32[4,128]{1,0:T(4,128)} %recv_ref.5) | copy-start | bytes 6148
  0.7 0.9 %copy-start.7 = (s32[3,128]{1,0:T(4,128)S(1)}, s32[3,128]{1,0:T(4,128)}, u32[]{:S(2)}) copy-start(s32[3,128]{1,0:T(4,128)} %send_ref.5) | copy-start | bytes 4612
  1.5 0.9 %copy-start = (f32[5,64,128]{2,1,0:T(8,128)S(1)}, f32[5,64,128]{2,1,0:T(8,128)}, u32[]{:S(2)}) copy-start(f32[5,64,128]{2,1,0:T(8,128)} %v_ref.3) | copy-start | bytes 491524
  2.4 28.1 %copy-start.1 = (f32[5,64,128]{2,1,0:T(8,128)S(1)}, f32[5,64,128]{2,1,0:T(8,128)}, u32[]{:S(2)}) copy-start(f32[5,64,128]{2,1,0:T(8,128)} %v_ref.3) | copy-start | bytes 491524
  3.6 26.9 %copy-start.2 = (bf16[256,192]{1,0:T(8,128)(2,1)S(1)}, bf16[256,192]{1,0:T(8,128)(2,1)}, u32[]{:S(2)}) copy-start(bf16[256,192]{1,0:T(8,128)(2,1)} %constant.6.clone.vt_ref) | copy-start | bytes 294916
  3.6 27.4 %all-to-all-start = ((f32[4,40,128]{2,1,0:T(8,128)}), f32[4,40,128]{2,1,0:T(8,128)S(1)}, u32[]{:S(2)}, u32[]{:S(2)}) async-start(f32[4,40,128]{2,1,0:T(8,128)} %get-tuple-element.17), calls=%async_computation | async-start | bytes 163840 | tf_op jit(solution)/shard_map/all_to_all | solution.py:291
  8.1 22.5 %copy-start.4 = (s32[6,128]{1,0:T(8,128)S(1)}, s32[6,128]{1,0:T(8,128)}, u32[]{:S(2)}) copy-start(s32[6,128]{1,0:T(8,128)} %nb_ref.7) | copy-start | bytes 9220
  8.1 23.0 %collective-permute-start = (f32[120,128]{1,0:T(8,128)S(1)}, f32[120,128]{1,0:T(8,128)S(1)}, u32[]{:S(2)}, u32[]{:S(2)}) collective-permute-start(f32[120,128]{1,0:T(8,128)S(1)} %get-tuple-element.15), channel_id=1, source_target_pairs={{0,1},{1,2},{2,3},{3,4},{4,5},{5,6},{6,7},{7,8},{8,9},{9,10},{10,1... | collective-permute-start | bytes 184328 | tf_op jit(solution)/shard_map/ppermute | solution.py:292
  12.1 18.4 %copy-start.9 = (f32[128]{0:T(128)S(1)}, f32[128]{0:T(128)}, u32[]{:S(2)}) copy-start(f32[128]{0:T(128)} %visc_ref.3) | copy-start | bytes 1540
  12.1 20.3 %collective-permute-start.1 = (f32[120,128]{1,0:T(8,128)S(1)}, f32[120,128]{1,0:T(8,128)S(1)}, u32[]{:S(2)}, u32[]{:S(2)}) collective-permute-start(f32[120,128]{1,0:T(8,128)S(1)} %get-tuple-element.16), channel_id=1, source_target_pairs={{1,0},{2,1},{3,2},{4,3},{5,4},{6,5},{7,6},{8,7},{9,8},{10,9},{11,1... | collective-permute-start | bytes 184328 | tf_op jit(solution)/shard_map/ppermute | solution.py:293
  30.6 1.8 %copy-start.5 = (bf16[64,48]{1,0:T(8,128)(2,1)S(1)}, bf16[64,48]{1,0:T(8,128)(2,1)}, u32[]{:S(2)}) copy-start(bf16[64,48]{1,0:T(8,128)(2,1)} %constant.8.clone.pt_ref) | copy-start | bytes 18436
  34.3 13.9 %copy-start.3 = (f32[5,64,128]{2,1,0:T(8,128)S(1)}, f32[5,64,128]{2,1,0:T(8,128)}, u32[]{:S(2)}) copy-start(f32[5,64,128]{2,1,0:T(8,128)} %get-tuple-element.11.v_ref) | copy-start | bytes 491524
  34.3 14.4 %all-to-all-start.1 = ((f32[4,40,128]{2,1,0:T(8,128)}), f32[4,40,128]{2,1,0:T(8,128)S(1)}, u32[]{:S(2)}, u32[]{:S(2)}) async-start(f32[4,40,128]{2,1,0:T(8,128)} %get-tuple-element.23), calls=%async_computation.1 | async-start | bytes 163840 | tf_op jit(solution)/shard_map/all_to_all | solution.py:291
  37.7 11.0 %collective-permute-start.2 = (f32[120,128]{1,0:T(8,128)S(1)}, f32[120,128]{1,0:T(8,128)S(1)}, u32[]{:S(2)}, u32[]{:S(2)}) collective-permute-start(f32[120,128]{1,0:T(8,128)S(1)} %get-tuple-element.21), channel_id=1, source_target_pairs={{0,1},{1,2},{2,3},{3,4},{4,5},{5,6},{6,7},{7,8},{8,9},{9,10},{10,1... | collective-permute-start | bytes 184328 | tf_op jit(solution)/shard_map/ppermute | solution.py:292
  41.6 8.4 %collective-permute-start.3 = (f32[120,128]{1,0:T(8,128)S(1)}, f32[120,128]{1,0:T(8,128)S(1)}, u32[]{:S(2)}, u32[]{:S(2)}) collective-permute-start(f32[120,128]{1,0:T(8,128)S(1)} %get-tuple-element.22), channel_id=1, source_target_pairs={{1,0},{2,1},{3,2},{4,3},{5,4},{6,5},{7,6},{8,7},{9,8},{10,9},{11,1... | collective-permute-start | bytes 184328 | tf_op jit(solution)/shard_map/ppermute | solution.py:293
where the time goes:
time: 51.8 us; the launch traced here: 51.3 us
  starting transfers between devices  40.8 us (79%)
  Pallas kernels  5.33 us (10%)
  waiting for transfers between devices  2.65 us (5%)
  local copies, waits for them, and re-layouts  1.78 us (3%)
  between operations  0.82 us (2%)
    ppermute x2, starting transfers between devices, exchange(): after = lax.ppermute(down, AXES, back)  25 us
    ppermute x2, starting transfers between devices, exchange(): before = lax.ppermute(up, AXES, onward)  7.93 us
    all_to_all x2, starting transfers between devices, exchange(): lax.all_to_all(mortar, 'group', split_axis=0, concat_axis=0, tiled=True)  7.85 us
    pallas_call x5, Pallas kernels, call(): pl.pallas_call(kernel, out_shape=outs, compiler_params=pltpu.CompilerPara...  5.33 us
    ppermute x2, waiting for transfers between devices, exchange(): after = lax.ppermute(down, AXES, back)  2.64 us
    unnamed x21, local copies, waits for them, and re-layouts  1.78 us
  transfers between devices with their start and end apart: 6, of which 2 were waited for; matrix products, arithmetic and copies ran while one was open for 0% of the time, Pallas kernels for 2%

commit v1 on v0

--- a/solution.py
+++ b/solution.py
@@ -1,5 +1,3 @@
-import functools
-
 import jax
 import jax.numpy as jnp
 import ml_dtypes
@@ -129,28 +127,34 @@
         o_ref[a, 48 * s : 48 * s + 16, :] += values
 
 
-def trace_part(v_ref, j_ref, send_ref, recv_ref, it_ref, g_ref, loc_ref, up_ref, down_ref, m_ref):
-    gs, hs = [], []
+def trace_part(v_ref, j_ref, g_ref, edge_ref):
     for f in range(6):
-        normal = 2.0 * (f % 2) - 1.0
+        d = f // 2
         w = [face_values(v_ref, f, b) for b in range(5)]
-        g_rows, h_rows = [], []
         for a in range(5):
-            q = j_ref[f // 2, a, 0:1, :] * w[0]
+            q = j_ref[a, 0, d : d + 1, :] * w[0]
             for b in range(1, 5):
-                q = q + j_ref[f // 2, a, b : b + 1, :] * w[b]
-            q = normal * q
-            g_rows.append(w[a] + q)
-            h_rows.append(w[a] - q)
-        gs.append(jnp.concatenate(g_rows, axis=0))
-        hs.append(jnp.concatenate(h_rows, axis=0))
-        g_ref[f] = gs[f]
+                q = q + j_ref[a, b, d : d + 1, :] * w[b]
+            g_ref[f, 16 * a : 16 * a + 16, :] = w[a] + q if f % 2 else w[a] - q
+    up, down = rims(g_ref)
+    edge_ref[...] = jnp.where(lax.axis_index("group") == 0, down, up)
+
+
+def rims(g_ref):
+    odd = jnp.concatenate([g_ref[1], g_ref[3], g_ref[5]], axis=0)
+    even = jnp.concatenate([g_ref[0], g_ref[2], g_ref[4]], axis=0)
     lane = lax.broadcasted_iota(jnp.int32, (120, 128), 1)
-    odd = jnp.concatenate([gs[1], gs[3], gs[5]], axis=0)
-    even = jnp.concatenate([gs[0], gs[2], gs[4]], axis=0)
-    up_ref[...] = jnp.where(lane < 64, pltpu.roll(odd[:120], 64, 1), odd[120:])
-    down_ref[...] = jnp.where(lane < 64, even[:120], pltpu.roll(even[120:], 64, 1))
-    hots = slot_one_hots(send_ref, recv_ref)
+    up = jnp.where(lane < 64, pltpu.roll(odd[:120], 64, 1), odd[120:])
+    down = jnp.where(lane < 64, even[:120], pltpu.roll(even[120:], 64, 1))
+    return up, down
+
+
+def mortar_part(v_ref, g_ref, hots, recv_ref, it_ref, loc_ref, m_ref):
+    gs = [g_ref[f] for f in range(6)]
+    ws = [
+        jnp.concatenate([face_values(v_ref, f, a) for a in range(5)], axis=0) for f in range(6)
+    ]
+    hs = [2.0 * ws[f] - gs[f] for f in range(6)]
     g_hi, g_lo = split(jnp.concatenate(gs, axis=1))
     h_hi, h_lo = split(jnp.concatenate(hs, axis=1))
     picked = dot(jnp.concatenate([g_hi, g_lo, h_hi, h_lo], axis=0), hots)
@@ -166,6 +170,8 @@
     loc_ref[...] = jnp.concatenate([h_inter, h_fine], axis=0)
     outgoing = jnp.concatenate([g_fine, g_inter], axis=0)
     quarter = lax.broadcasted_iota(jnp.int32, (40, 128), 1) // 32
+    up, down = rims(g_ref)
+    me = lax.axis_index("group")
     for t in range(4):
         block = None
         for q in range(4):
@@ -173,21 +179,33 @@
             shift = (32 * (q - t)) % 128
             part = pltpu.roll(part, shift, 1) if shift else part
             block = part if block is None else jnp.where(quarter == q, part, block)
-        m_ref[t] = block
-
-
-def combine_part(
-    base_ref, g_ref, loc_ref, before_ref, after_ref, m_ref, nb_ref, send_ref, recv_ref, pt_ref, o_ref
-):
+        m_ref[t, 0:40, :] = block
+        m_ref[t, 40:160, :] = jnp.where(me < t, up, down)
+
+
+def conforming_one_hots(nb_ref, hot_ref):
     first_id = (lax.axis_index("curve") * 4 + lax.axis_index("group")) * 128
+    for f in range(6):
+        linked = nb_ref[f : f + 1, :]
+        place = linked - first_id
+        if f % 2 == 0:
+            place = jnp.where(place < 0, place + 192, place)
+        hot_ref[f] = one_hot(jnp.where(linked < 0, -1, place), 256)
+
+
+def combine_part(base_ref, g_ref, loc_ref, edge_ref, m_ref, hot_ref, slot_ref, recv_ref, pt_ref, o_ref):
+    me = lax.axis_index("group")
     o_ref[...] = base_ref[...]
+    edge = edge_ref[...]
+    before = jnp.where(me == 0, edge, m_ref[jnp.maximum(me - 1, 0), 40:160, :])
+    after = jnp.where(me == 3, edge, m_ref[jnp.minimum(me + 1, 3), 40:160, :])
     quarter = lax.broadcasted_iota(jnp.int32, (40, 128), 1) // 32
     parts = []
     for q in range(4):
         part = None
         for s in range(4):
             shift = (32 * (s - q)) % 128
-            block = m_ref[s]
+            block = m_ref[s, 0:40, :]
             block = pltpu.roll(block, shift, 1) if shift else block
             part = block if part is None else jnp.where(quarter == s, block, part)
         parts.append(part)
@@ -195,41 +213,28 @@
     projected = by_child(pt_ref, [incoming[16 * a : 16 * a + 16] for a in range(5)], recv_ref)
     values = jnp.concatenate([incoming[80:160], jnp.concatenate(projected, axis=0)], axis=1)
     hi, lo = split(values)
-    hots = slot_one_hots(send_ref, recv_ref)
     spread = lax.dot_general(
         jnp.concatenate([hi, lo], axis=0),
-        hots,
+        slot_ref[...],
         (((1,), (1,)), ((), ())),
         preferred_element_type=F32,
     )
     mortar = spread[0:80] + spread[80:160]
-    before, after = before_ref[...], after_ref[...]
     before = jnp.concatenate([before, pltpu.roll(before, 64, 1)], axis=0)
     after = jnp.concatenate([after, pltpu.roll(after, 64, 1)], axis=0)
     for f in range(6):
-        linked = nb_ref[f : f + 1, :]
-        place = linked - first_id
-        if f % 2 == 0:
-            halo = before
-            place = jnp.where(place < 0, place + 192, place)
-        else:
-            halo = after
-        place = jnp.where(linked < 0, -1, place)
+        halo = after if f % 2 else before
         third = f // 2
         source = jnp.concatenate([g_ref[f ^ 1], halo[80 * third : 80 * third + 80]], axis=1)
         hi, lo = split(source)
-        far = dot(jnp.concatenate([hi, lo], axis=0), one_hot(place, 256))
+        far = dot(jnp.concatenate([hi, lo], axis=0), hot_ref[f])
         total = far[0:80] + far[80:160] + mortar[:, 128 * f : 128 * f + 128]
         total = total * (-FACE_SCALE)
         for a in range(5):
             add_to_face(o_ref, f, a, total[16 * a : 16 * a + 16])
 
 
-def trace_kernel(v_ref, j_ref, send_ref, recv_ref, it_ref, g_ref, loc_ref, up_ref, down_ref, m_ref):
-    trace_part(v_ref, j_ref, send_ref, recv_ref, it_ref, g_ref, loc_ref, up_ref, down_ref, m_ref)
-
-
-def volume_kernel(v_ref, j_ref, visc_ref, nb_ref, g_ref, vt_ref, o_ref):
+def volume_part(v_ref, j_ref, visc_ref, nb_ref, g_ref, vt_ref, o_ref):
     v = v_ref[...]
     hi, lo = split(jnp.concatenate([v[a] for a in range(5)], axis=1))
     terms = dot(vt_ref[...], jnp.concatenate([hi, lo, hi], axis=0))
@@ -238,7 +243,7 @@
         total = visc * terms[192:256, 128 * a : 128 * a + 128]
         for d in range(3):
             for b in range(5):
-                total = total - j_ref[d, a, b : b + 1, :] * terms[
+                total = total - j_ref[a, b, d : d + 1, :] * terms[
                     64 * d : 64 * d + 64, 128 * b : 128 * b + 128
                 ]
         o_ref[a] = v[a] - PSEUDO_STEP * total
@@ -249,27 +254,39 @@
             add_to_face(o_ref, f, a, mask * h)
 
 
-def middle_kernel(
-    base_ref, g_ref, loc_ref, before_ref, after_ref, m_ref, nb_ref, send_ref, recv_ref,
-    j_ref, it_ref, pt_ref,
-    o_ref, g2_ref, loc2_ref, up_ref, down_ref, m2_ref,
+def first_traces(v_ref, j_ref, g_ref, edge_ref):
+    trace_part(v_ref, j_ref, g_ref, edge_ref)
+
+
+def first_mortars(v_ref, g_ref, send_ref, recv_ref, it_ref, loc_ref, m_ref, slot_ref):
+    hots = slot_one_hots(send_ref, recv_ref)
+    slot_ref[...] = hots
+    mortar_part(v_ref, g_ref, hots, recv_ref, it_ref, loc_ref, m_ref)
+
+
+def second_mortars(v_ref, g_ref, slot_ref, recv_ref, it_ref, loc_ref, m_ref):
+    mortar_part(v_ref, g_ref, slot_ref[...], recv_ref, it_ref, loc_ref, m_ref)
+
+
+def first_volume(v_ref, j_ref, visc_ref, nb_ref, g_ref, vt_ref, o_ref, hot_ref):
+    volume_part(v_ref, j_ref, visc_ref, nb_ref, g_ref, vt_ref, o_ref)
+    conforming_one_hots(nb_ref, hot_ref)
+
+
+def second_volume(v_ref, j_ref, visc_ref, nb_ref, g_ref, vt_ref, o_ref):
+    volume_part(v_ref, j_ref, visc_ref, nb_ref, g_ref, vt_ref, o_ref)
+
+
+def middle(
+    base_ref, g_ref, loc_ref, edge_ref, m_ref, hot_ref, slot_ref, recv_ref, pt_ref, j_ref,
+    o_ref, g2_ref, edge2_ref,
 ):
-    combine_part(
-        base_ref, g_ref, loc_ref, before_ref, after_ref, m_ref, nb_ref, send_ref, recv_ref, pt_ref, o_ref
-    )
-    trace_part(o_ref, j_ref, send_ref, recv_ref, it_ref, g2_ref, loc2_ref, up_ref, down_ref, m2_ref)
-
-
-def final_kernel(
-    base_ref, g_ref, loc_ref, before_ref, after_ref, m_ref, nb_ref, send_ref, recv_ref, pt_ref, o_ref
-):
-    combine_part(
-        base_ref, g_ref, loc_ref, before_ref, after_ref, m_ref, nb_ref, send_ref, recv_ref, pt_ref, o_ref
-    )
-
-
-def shape(*dims):
-    return jax.ShapeDtypeStruct(dims, F32)
+    combine_part(base_ref, g_ref, loc_ref, edge_ref, m_ref, hot_ref, slot_ref, recv_ref, pt_ref, o_ref)
+    trace_part(o_ref, j_ref, g2_ref, edge2_ref)
+
+
+def shape(*dims, kind=F32):
+    return jax.ShapeDtypeStruct(dims, kind)
 
 
 def call(kernel, outs, *args):
@@ -280,43 +297,55 @@
     )(*args)
 
 
-IMAGE = (5, 64, 128)
-TRACES = (shape(6, 80, 128), shape(160, 128), shape(120, 128), shape(120, 128), shape(4, 40, 128))
-
-
-def exchange(up, down, mortar):
-    count = lax.axis_size(AXES)
-    onward = [(i, i + 1) for i in range(count - 1)]
-    back = [(i + 1, i) for i in range(count - 1)]
-    mortar = lax.all_to_all(mortar, "group", split_axis=0, concat_axis=0, tiled=True)
-    before = lax.ppermute(up, AXES, onward)
-    after = lax.ppermute(down, AXES, back)
-    return before, after, mortar
+IMAGE = shape(5, 64, 128)
+TRACES = shape(6, 80, 128)
+EDGE = shape(120, 128)
+SLOTS = shape(160, 128)
+MESSAGE = shape(4, 160, 128)
+SLOT_HOTS = shape(768, 256, kind=BF16)
+FACE_HOTS = shape(6, 256, 128, kind=BF16)
+
+
+def swap_edges(edge):
+    ends = [(4 * c + 3, 4 * c + 4) for c in range(lax.axis_size("curve") - 1)]
+    return lax.ppermute(edge, AXES, ends + [(j, i) for i, j in ends])
+
+
+def exchange(message):
+    return lax.all_to_all(message, "group", split_axis=0, concat_axis=0, tiled=True)
 
 
 def local(tangent, jacobian, viscosity, neighbours, send_table, recv_table):
     volume_table, inter_table, project_table = (jnp.asarray(t) for t in operator_tables())
-    g, loc, up, down, mortar = call(
-        trace_kernel, TRACES, tangent, jacobian, send_table, recv_table, inter_table
-    )
-    before, after, mortar = exchange(up, down, mortar)
+    jacobian = jnp.transpose(jacobian, (1, 2, 0, 3))
+    g, edge = call(first_traces, (TRACES, EDGE), tangent, jacobian)
+    edge = swap_edges(edge)
+    loc, message, slots = call(
+        first_mortars, (SLOTS, MESSAGE, SLOT_HOTS), tangent, g, send_table, recv_table, inter_table
+    )
+    message = exchange(message)
+    base, hots = call(
+        first_volume,
+        (IMAGE, FACE_HOTS),
+        tangent, jacobian, viscosity, neighbours, g, volume_table,
+    )
+    first, g, edge = call(
+        middle,
+        (IMAGE, TRACES, EDGE),
+        base, g, loc, edge, message, hots, slots, recv_table, project_table, jacobian,
+    )
+    edge = swap_edges(edge)
+    loc, message = call(
+        second_mortars, (SLOTS, MESSAGE), first, g, slots, recv_table, inter_table
+    )
+    message = exchange(message)
     base = call(
-        volume_kernel, shape(*IMAGE), tangent, jacobian, viscosity, neighbours, g, volume_table
-    )
-    first, g, loc, up, down, mortar = call(
-        middle_kernel,
-        (shape(*IMAGE),) + TRACES,
-        base, g, loc, before, after, mortar, neighbours, send_table, recv_table,
-        jacobian, inter_table, project_table,
-    )
-    before, after, mortar = exchange(up, down, mortar)
-    base = call(
-        volume_kernel, shape(*IMAGE), first, jacobian, viscosity, neighbours, g, volume_table
+        second_volume, IMAGE, first, jacobian, viscosity, neighbours, g, volume_table
     )
     second = call(
-        final_kernel,
-        shape(*IMAGE),
-        base, g, loc, before, after, mortar, neighbours, send_table, recv_table, project_table,
+        combine_part,
+        IMAGE,
+        base, g, loc, edge, message, hots, slots, recv_table, project_table,
     )
     return first, second
 

time: 51.8 us -> 50.1 us (0.967)
  starting transfers between devices: 40.8 us -> 36.8 us
  local copies, waits for them, and re-layouts: 1.78 us -> 3.25 us
  Pallas kernels: 5.33 us -> 6.26 us
    ppermute x4 -> x2, starting transfers between devices: 32.9 us -> 28.9 us  [swap_edges(): return lax.ppermute(edge, AXES, ends + [(j, i) for i, j in ends])]
    unnamed x21 -> x24, local copies, waits for them, and re-layouts: 1.78 us -> 3.25 us
    pallas_call x5 -> x7, Pallas kernels: 5.33 us -> 6.26 us  [call(): pl.pallas_call(kernel, out_shape=outs, compiler_params=pltpu.CompilerPara...]
    ppermute x4 -> x2, waiting for transfers between devices: 2.64 us -> 2.66 us  [swap_edges(): return lax.ppermute(edge, AXES, ends + [(j, i) for i, j in ends])]
  transfers between devices with their start and end apart: 6 -> 4, of which waited for: 2 -> 2; matrix products, arithmetic and copies ran while one was open for 0% -> 0% of each run, Pallas kernels for 2% -> 2%
where the time goes in v1:
time: 50.1 us; the launch traced here: 49.7 us
  starting transfers between devices  36.8 us (73%)
  Pallas kernels  6.26 us (12%)
  local copies, waits for them, and re-layouts  3.25 us (6%)
  waiting for transfers between devices  2.66 us (5%)
  between operations  0.73 us (1%)
    ppermute x2, starting transfers between devices, swap_edges(): return lax.ppermute(edge, AXES, ends + [(j, i) for i, j in ends])  28.9 us
    all_to_all x2, starting transfers between devices, exchange(): lax.all_to_all(message, 'group', split_axis=0, concat_axis=0, tiled=True)  7.89 us
    pallas_call x7, Pallas kernels, call(): pl.pallas_call(kernel, out_shape=outs, compiler_params=pltpu.CompilerPara...  6.26 us
    unnamed x24, local copies, waits for them, and re-layouts  3.25 us
    ppermute x2, waiting for transfers between devices, swap_edges(): return lax.ppermute(edge, AXES, ends + [(j, i) for i, j in ends])  2.66 us
  transfers between devices with their start and end apart: 4, of which 2 were waited for; matrix products, arithmetic and copies ran while one was open for 0% of the time, Pallas kernels for 2%

profile of v1, /device:TPU:24, one launch (start us, length us, event | category | flops | bytes accessed | tf_op | source)
XLA Modules:
  0.0 49.7 jit_solution(11744818099594854002)
XLA Ops:
  0.6 0.0 copy-start
  0.6 0.9 %copy-done = f32[5,64,128]{2,1,0:T(8,128)S(1)} copy-done((f32[5,64,128]{2,1,0:T(8,128)S(1)}, f32[5,64,128]{2,1,0:T(8,128)}, u32[]{:S(2)}) %copy-start) | copy-done | bytes 163864
  1.5 0.0 copy-start.2
  1.6 0.8 %copy-done.2 = f32[3,5,5,128]{3,0,2,1:T(4,128)S(1)} copy-done((f32[3,5,5,128]{3,0,2,1:T(4,128)S(1)}, f32[3,5,5,128]{3,0,2,1:T(4,128)}, u32[]{:S(2)}) %copy-start.2) | copy-done | bytes 38424
  2.4 0.0 copy-start.7
  2.4 0.0 copy-start.8
  2.4 0.0 copy-start.10
  2.4 0.1 shard_map.104
  2.5 0.6 %copy-done.7 = bf16[64,48]{1,0:T(8,128)(2,1)S(1)} copy-done((bf16[64,48]{1,0:T(8,128)(2,1)S(1)}, bf16[64,48]{1,0:T(8,128)(2,1)}, u32[]{:S(2)}) %copy-start.7) | copy-done | bytes 6168
  3.1 0.0 copy-done.8
  3.1 0.0 copy-done.10
  3.1 1.3 %shard_map.106 = (f32[160,128]{1,0:T(8,128)S(1)}, f32[4,160,128]{2,1,0:T(8,128)}, bf16[768,256]{1,0:T(8,128)(2,1)S(1)}) custom-call(f32[5,64,128]{2,1,0:T(8,128)S(1)} %copy-done, f32[6,80,128]{2,1,0:T(8,128)S(1)} %get-tuple-element.14.g_ref, s32[3,128]{1,0:T(4,128)S(1)} %copy-done.10, s32[4,128]{1,0:T(4,128)S(1)} %copy-done.8, bf16[64,48]{1,0:T(8,128)(2,1)S(1)} %copy-done.7), custom_call_target="tpu_custom_call" | custom-call | tf_op jit(solution)/shard_map/pallas_call | solution.py:293
  4.3 0.0 copy-start.1
  4.3 0.0 copy-start.3
  4.3 0.0 copy-start.5
  4.3 0.0 copy-start.9
  4.3 4.4 %all-to-all-start = ((f32[4,160,128]{2,1,0:T(8,128)}), f32[4,160,128]{2,1,0:T(8,128)S(1)}, u32[]{:S(2)}, u32[]{:S(2)}) async-start(f32[4,160,128]{2,1,0:T(8,128)} %get-tuple-element.18), calls=%async_computation | async-start | bytes 655360 | tf_op jit(solution)/shard_map/all_to_all | solution.py:315
  8.8 0.0 copy-start.11
  8.8 20.5 %collective-permute-start = (f32[120,128]{1,0:T(8,128)S(1)}, f32[120,128]{1,0:T(8,128)S(1)}, u32[]{:S(2)}, u32[]{:S(2)}) collective-permute-start(f32[120,128]{1,0:T(8,128)S(1)} %get-tuple-element.17), channel_id=1, source_target_pairs={{3,4},{7,8},{11,12},{15,16},{19,20},{23,24},{27,28},{31,32},{35,36... | collective-permute-start | bytes 184328 | tf_op jit(solution)/shard_map/ppermute | solution.py:311
  29.3 0.0 copy-done.1
  29.3 0.0 copy-done.3
  29.3 0.0 copy-done.5
  29.3 0.0 copy-done.9
  29.4 0.0 copy-done.11
  29.4 0.0 copy-start.6
  29.4 0.6 %shard_map.105 = (f32[5,64,128]{2,1,0:T(8,128)S(1)}, bf16[6,256,128]{2,1,0:T(8,128)(2,1)S(1)}) custom-call(f32[5,64,128]{2,1,0:T(8,128)S(1)} %copy-done.1, f32[5,5,3,128]{3,2,1,0:T(4,128)S(1)} %bitcast.2, f32[128]{0:T(128)S(1)} %copy-done.11, s32[6,128]{1,0:T(8,128)S(1)} %copy-done.9, f32[6,80,128]{2,1,0:T(8,128)S(1)} %get-tuple-element.14.g_ref, ...), custom_call_target="tpu_custom_call" | custom-call | tf_op jit(solution)/shard_map/pallas_call | solution.py:293
  30.0 1.2 %collective-permute-done.edge_ref = f32[120,128]{1,0:T(8,128)S(1)} collective-permute-done((f32[120,128]{1,0:T(8,128)S(1)}, f32[120,128]{1,0:T(8,128)S(1)}, u32[]{:S(2)}, u32[]{:S(2)}) %collective-permute-start) | collective-permute-done | bytes 61472 | tf_op jit(solution)/shard_map/ppermute | solution.py:311
  31.2 0.0 all-to-all-done.m_ref
  31.2 0.0 copy-done.6
  31.2 1.3 %shard_map.107 = (f32[5,64,128]{2,1,0:T(8,128)}, f32[6,80,128]{2,1,0:T(8,128)S(1)}, f32[120,128]{1,0:T(8,128)S(1)}) custom-call(f32[5,64,128]{2,1,0:T(8,128)S(1)} %get-tuple-element.15.base_ref, f32[6,80,128]{2,1,0:T(8,128)S(1)} %get-tuple-element.14.g_ref, f32[160,128]{1,0:T(8,128)S(1)} %get-tuple-element.16.loc_ref, ...), custom_call_target="tpu_custom_call" | custom-call | tf_op jit(solution)/shard_map/pallas_call | solution.py:293
  32.5 0.0 copy-start.4
  32.5 0.9 %copy-done.4 = f32[5,64,128]{2,1,0:T(8,128)S(1)} copy-done((f32[5,64,128]{2,1,0:T(8,128)S(1)}, f32[5,64,128]{2,1,0:T(8,128)}, u32[]{:S(2)}) %copy-start.4) | copy-done | bytes 163864
  33.4 1.2 %shard_map.109 = (f32[160,128]{1,0:T(8,128)S(1)}, f32[4,160,128]{2,1,0:T(8,128)}) custom-call(f32[5,64,128]{2,1,0:T(8,128)S(1)} %copy-done.4, f32[6,80,128]{2,1,0:T(8,128)S(1)} %get-tuple-element.22.g_ref, bf16[768,256]{1,0:T(8,128)(2,1)S(1)} %get-tuple-element.20.slot_ref, s32[4,128]{1,0:T(4,128)S(1)} %copy-done.8, bf16[64,48]{1,0:T(8,128)(2,1)S(1)} %copy-done.7), custom_call_target="tpu_custom_call" | custom-call | tf_op jit(solution)/shard_map/pallas_call | solution.py:293
  34.7 3.5 %all-to-all-start.1 = ((f32[4,160,128]{2,1,0:T(8,128)}), f32[4,160,128]{2,1,0:T(8,128)S(1)}, u32[]{:S(2)}, u32[]{:S(2)}) async-start(f32[4,160,128]{2,1,0:T(8,128)} %get-tuple-element.25), calls=%async_computation.1 | async-start | bytes 655360 | tf_op jit(solution)/shard_map/all_to_all | solution.py:315
  38.1 8.3 %collective-permute-start.1 = (f32[120,128]{1,0:T(8,128)S(1)}, f32[120,128]{1,0:T(8,128)S(1)}, u32[]{:S(2)}, u32[]{:S(2)}) collective-permute-start(f32[120,128]{1,0:T(8,128)S(1)} %get-tuple-element.24), channel_id=1, source_target_pairs={{3,4},{7,8},{11,12},{15,16},{19,20},{23,24},{27,28},{31,32},{35,36... | collective-permute-start | bytes 184328 | tf_op jit(solution)/shard_map/ppermute | solution.py:311
  46.5 0.5 shard_map.108.base_ref
  46.9 1.4 %collective-permute-done.1.edge_ref = f32[120,128]{1,0:T(8,128)S(1)} collective-permute-done((f32[120,128]{1,0:T(8,128)S(1)}, f32[120,128]{1,0:T(8,128)S(1)}, u32[]{:S(2)}, u32[]{:S(2)}) %collective-permute-start.1) | collective-permute-done | bytes 61472 | tf_op jit(solution)/shard_map/ppermute | solution.py:311
  48.4 0.0 all-to-all-done.1.m_ref
  48.4 1.3 %shard_map.110 = f32[5,64,128]{2,1,0:T(8,128)} custom-call(f32[5,64,128]{2,1,0:T(8,128)S(1)} %shard_map.108.base_ref, f32[6,80,128]{2,1,0:T(8,128)S(1)} %get-tuple-element.22.g_ref, f32[160,128]{1,0:T(8,128)S(1)} %get-tuple-element.23.loc_ref, f32[120,128]{1,0:T(8,128)S(1)} %collective-permute-done.1.edge_ref, f32[4,160,128]{2,1,0:T(8,128)S(1)} %all-to-all-done.1.m_ref, ...), custom_call_target="tpu_custom_call" | custom-call | tf_op jit(solution)/shard_map/pallas_call | solution.py:293
Async XLA Ops:
  0.6 0.9 %copy-start = (f32[5,64,128]{2,1,0:T(8,128)S(1)}, f32[5,64,128]{2,1,0:T(8,128)}, u32[]{:S(2)}) copy-start(f32[5,64,128]{2,1,0:T(8,128)} %v_ref.5) | copy-start | bytes 491524
  1.5 0.8 %copy-start.2 = (f32[3,5,5,128]{3,0,2,1:T(4,128)S(1)}, f32[3,5,5,128]{3,0,2,1:T(4,128)}, u32[]{:S(2)}) copy-start(f32[3,5,5,128]{3,0,2,1:T(4,128)} %param.10) | copy-start | bytes 115204
  2.4 0.7 %copy-start.7 = (bf16[64,48]{1,0:T(8,128)(2,1)S(1)}, bf16[64,48]{1,0:T(8,128)(2,1)}, u32[]{:S(2)}) copy-start(bf16[64,48]{1,0:T(8,128)(2,1)} %constant.7.clone.it_ref) | copy-start | bytes 18436
  2.4 0.7 %copy-start.8 = (s32[4,128]{1,0:T(4,128)S(1)}, s32[4,128]{1,0:T(4,128)}, u32[]{:S(2)}) copy-start(s32[4,128]{1,0:T(4,128)} %recv_ref.7) | copy-start | bytes 6148
  2.4 0.7 %copy-start.10 = (s32[3,128]{1,0:T(4,128)S(1)}, s32[3,128]{1,0:T(4,128)}, u32[]{:S(2)}) copy-start(s32[3,128]{1,0:T(4,128)} %send_ref.1) | copy-start | bytes 4612
  4.3 25.0 %copy-start.1 = (f32[5,64,128]{2,1,0:T(8,128)S(1)}, f32[5,64,128]{2,1,0:T(8,128)}, u32[]{:S(2)}) copy-start(f32[5,64,128]{2,1,0:T(8,128)} %v_ref.5) | copy-start | bytes 491524
  4.3 25.0 %copy-start.3 = (f32[3,5,5,128]{3,0,2,1:T(4,128)S(1)}, f32[3,5,5,128]{3,0,2,1:T(4,128)}, u32[]{:S(2)}) copy-start(f32[3,5,5,128]{3,0,2,1:T(4,128)} %param.10) | copy-start | bytes 115204
  4.3 25.0 %copy-start.5 = (bf16[256,192]{1,0:T(8,128)(2,1)S(1)}, bf16[256,192]{1,0:T(8,128)(2,1)}, u32[]{:S(2)}) copy-start(bf16[256,192]{1,0:T(8,128)(2,1)} %constant.6.clone.vt_ref) | copy-start | bytes 294916
  4.3 25.0 %copy-start.9 = (s32[6,128]{1,0:T(8,128)S(1)}, s32[6,128]{1,0:T(8,128)}, u32[]{:S(2)}) copy-start(s32[6,128]{1,0:T(8,128)} %nb_ref.3) | copy-start | bytes 9220
  4.3 26.9 %all-to-all-start = ((f32[4,160,128]{2,1,0:T(8,128)}), f32[4,160,128]{2,1,0:T(8,128)S(1)}, u32[]{:S(2)}, u32[]{:S(2)}) async-start(f32[4,160,128]{2,1,0:T(8,128)} %get-tuple-element.18), calls=%async_computation | async-start | bytes 655360 | tf_op jit(solution)/shard_map/all_to_all | solution.py:315
  8.8 20.6 %copy-start.11 = (f32[128]{0:T(128)S(1)}, f32[128]{0:T(128)}, u32[]{:S(2)}) copy-start(f32[128]{0:T(128)} %visc_ref.3) | copy-start | bytes 1540
  8.8 22.4 %collective-permute-start = (f32[120,128]{1,0:T(8,128)S(1)}, f32[120,128]{1,0:T(8,128)S(1)}, u32[]{:S(2)}, u32[]{:S(2)}) collective-permute-start(f32[120,128]{1,0:T(8,128)S(1)} %get-tuple-element.17), channel_id=1, source_target_pairs={{3,4},{7,8},{11,12},{15,16},{19,20},{23,24},{27,28},{31,32},{35,36... | collective-permute-start | bytes 184328 | tf_op jit(solution)/shard_map/ppermute | solution.py:311
  29.4 1.8 %copy-start.6 = (bf16[64,48]{1,0:T(8,128)(2,1)S(1)}, bf16[64,48]{1,0:T(8,128)(2,1)}, u32[]{:S(2)}) copy-start(bf16[64,48]{1,0:T(8,128)(2,1)} %constant.8.clone.pt_ref) | copy-start | bytes 18436
  32.5 0.9 %copy-start.4 = (f32[5,64,128]{2,1,0:T(8,128)S(1)}, f32[5,64,128]{2,1,0:T(8,128)}, u32[]{:S(2)}) copy-start(f32[5,64,128]{2,1,0:T(8,128)} %get-tuple-element.12.v_ref) | copy-start | bytes 491524
  34.7 13.7 %all-to-all-start.1 = ((f32[4,160,128]{2,1,0:T(8,128)}), f32[4,160,128]{2,1,0:T(8,128)S(1)}, u32[]{:S(2)}, u32[]{:S(2)}) async-start(f32[4,160,128]{2,1,0:T(8,128)} %get-tuple-element.25), calls=%async_computation.1 | async-start | bytes 655360 | tf_op jit(solution)/shard_map/all_to_all | solution.py:315
  38.1 10.2 %collective-permute-start.1 = (f32[120,128]{1,0:T(8,128)S(1)}, f32[120,128]{1,0:T(8,128)S(1)}, u32[]{:S(2)}, u32[]{:S(2)}) collective-permute-start(f32[120,128]{1,0:T(8,128)S(1)} %get-tuple-element.24), channel_id=1, source_target_pairs={{3,4},{7,8},{11,12},{15,16},{19,20},{23,24},{27,28},{31,32},{35,36... | collective-permute-start | bytes 184328 | tf_op jit(solution)/shard_map/ppermute | solution.py:311

commit v2 on v1

v2 whole, which is shorter than its diff:
```python
import jax
import jax.numpy as jnp
import ml_dtypes
import numpy as np
from jax import lax
from jax.experimental import pallas as pl
from jax.experimental.pallas import tpu as pltpu
from jax.sharding import PartitionSpec as P

F32 = jnp.float32
BF16 = jnp.bfloat16
AXES = ("curve", "group")
PSEUDO_STEP = 0.05
FACE_SCALE = 0.15


def node_tables():
    points = np.array([-1.0, -1.0 / np.sqrt(5.0), 1.0 / np.sqrt(5.0), 1.0])
    weights = np.array([1.0, 5.0, 5.0, 1.0]) / 6.0
    barycentric = np.array(
        [1.0 / np.prod([points[j] - points[k] for k in range(4) if k != j]) for j in range(4)]
    )
    derivative = np.zeros((4, 4))
    for a in range(4):
        for b in range(4):
            if a != b:
                derivative[a, b] = barycentric[b] / barycentric[a] / (points[a] - points[b])
        derivative[a, a] = -np.sum(derivative[a])
    halves = []
    for upper_half in range(2):
        matrix = np.zeros((4, 4))
        for a in range(4):
            target = 0.5 * points[a] + upper_half - 0.5
            for b in range(4):
                matrix[a, b] = np.prod(
                    [(target - points[k]) / (points[b] - points[k]) for k in range(4) if k != b]
                )
        halves.append(matrix)
    surface_weights = np.kron(weights, weights)
    interpolate = np.stack([np.kron(halves[c // 2], halves[c % 2]) for c in range(4)])
    project = np.stack(
        [
            0.25 * (interpolate[c].T * surface_weights[None, :]) / surface_weights[:, None]
            for c in range(4)
        ]
    )
    return derivative, interpolate, project


def pieces_of(matrix):
    hi = matrix.astype(ml_dtypes.bfloat16)
    lo = (matrix - hi.astype(np.float64)).astype(ml_dtypes.bfloat16)
    return np.concatenate([hi, hi, lo], axis=1)


def operator_tables():
    derivative, interpolate, project = node_tables()
    eye = np.eye(4)
    d_x = np.kron(eye, np.kron(eye, derivative))
    d_y = np.kron(eye, np.kron(derivative, eye))
    d_z = np.kron(derivative, np.kron(eye, eye))
    laplacian = d_x @ d_x + d_y @ d_y + d_z @ d_z
    volume = pieces_of(np.concatenate([d_x, d_y, d_z, laplacian], axis=0))
    return (
        volume,
        pieces_of(interpolate.reshape(64, 16)),
        pieces_of(project.reshape(64, 16)),
    )


def split(x):
    hi = x.astype(BF16)
    lo = (x - hi.astype(F32)).astype(BF16)
    return hi, lo


def dot(a, b):
    return lax.dot_general(a, b, (((1,), (0,)), ((), ())), preferred_element_type=F32)


def one_hot(index, rows):
    place = lax.broadcasted_iota(jnp.int32, (rows, index.shape[1]), 0)
    return jnp.where(place == index, 1.0, 0.0).astype(BF16)


def slot_one_hots(send_ref, recv_ref):
    fine = jnp.where(send_ref[2:3, :] > 0, send_ref[1:2, :] * 128 + send_ref[0:1, :], -1)
    coarse = jnp.where(recv_ref[3:4, :] > 0, recv_ref[1:2, :] * 128 + recv_ref[0:1, :], -1)
    return jnp.concatenate([one_hot(fine, 768), one_hot(coarse, 768)], axis=1)


def by_child(table_ref, values, recv_ref):
    count = len(values)
    hi, lo = split(jnp.concatenate(values, axis=1))
    product = dot(table_ref[...], jnp.concatenate([hi, lo, hi], axis=0))
    child = recv_ref[2:3, :]
    picks = [jnp.where(child == c, 1.0, 0.0) for c in range(4)]
    return [
        sum(
            product[16 * c : 16 * c + 16, 128 * n : 128 * n + 128] * picks[c]
            for c in range(4)
        )
        for n in range(count)
    ]


def face_values(v_ref, face, a):
    d, s = face // 2, face % 2
    if d == 0:
        return v_ref[a, pl.ds(3 * s, 16, stride=4), :]
    if d == 1:
        return jnp.concatenate(
            [v_ref[a, 16 * k + 12 * s : 16 * k + 12 * s + 4, :] for k in range(4)], axis=0
        )
    return v_ref[a, 48 * s : 48 * s + 16, :]


def add_to_face(o_ref, face, a, values):
    d, s = face // 2, face % 2
    if d == 0:
        o_ref[a, pl.ds(3 * s, 16, stride=4), :] += values
    elif d == 1:
        for k in range(4):
            row = 16 * k + 12 * s
            o_ref[a, row : row + 4, :] += values[4 * k : 4 * k + 4]
    else:
        o_ref[a, 48 * s : 48 * s + 16, :] += values


def rims(g_ref):
    odd = jnp.concatenate([g_ref[1], g_ref[3], g_ref[5]], axis=0)
    even = jnp.concatenate([g_ref[0], g_ref[2], g_ref[4]], axis=0)
    lane = lax.broadcasted_iota(jnp.int32, (120, 128), 1)
    up = jnp.where(lane < 64, pltpu.roll(odd[:120], 64, 1), odd[120:])
    down = jnp.where(lane < 64, even[:120], pltpu.roll(even[120:], 64, 1))
    return up, down


def trace_part(v_ref, j_ref, g_ref, h_ref):
    for f in range(6):
        d = f // 2
        w = [face_values(v_ref, f, b) for b in range(5)]
        for a in range(5):
            q = j_ref[a, 0, d : d + 1, :] * w[0]
            for b in range(1, 5):
                q = q + j_ref[a, b, d : d + 1, :] * w[b]
            rows = slice(16 * a, 16 * a + 16)
            plus, minus = (g_ref, h_ref) if f % 2 else (h_ref, g_ref)
            plus[f, rows, :] = w[a] + q
            minus[f, rows, :] = w[a] - q


def pick_slots(t_ref, hots):
    hi, lo = split(jnp.concatenate([t_ref[f] for f in range(6)], axis=1))
    picked = dot(jnp.concatenate([hi, lo], axis=0), hots)
    return picked[:80], picked[80:]


def inter_slots(values, it_ref, recv_ref):
    rows = [values[16 * a : 16 * a + 16] for a in range(5)]
    return jnp.concatenate(by_child(it_ref, rows, recv_ref), axis=0)


def send_part(g_ref, hots, recv_ref, it_ref, edge_ref, m_ref):
    me = lax.axis_index("group")
    up, down = rims(g_ref)
    edge_ref[...] = jnp.where(me == 0, down, up)
    hi, lo = pick_slots(g_ref, hots)
    picked = hi + lo
    outgoing = jnp.concatenate(
        [picked[:, :128], inter_slots(picked[:, 128:], it_ref, recv_ref)], axis=0
    )
    quarter = lax.broadcasted_iota(jnp.int32, (40, 128), 1) // 32
    for t in range(4):
        block = None
        for q in range(4):
            part = outgoing[40 * q : 40 * q + 40]
            shift = (32 * (q - t)) % 128
            part = pltpu.roll(part, shift, 1) if shift else part
            block = part if block is None else jnp.where(quarter == q, part, block)
        m_ref[t, 0:40, :] = block
        m_ref[t, 40:160, :] = jnp.where(me < t, up, down)


def places(nb_ref, f):
    first_id = (lax.axis_index("curve") * 4 + lax.axis_index("group")) * 128
    linked = nb_ref[f : f + 1, :]
    return linked >= 0, linked - first_id


def rim_one_hots(nb_ref, hot_ref):
    for f in range(6):
        linked, place = places(nb_ref, f)
        place = place - 128 if f % 2 else place + 64
        rim = linked & (place >= 0 if f % 2 else place < 64)
        hot = one_hot(jnp.where(rim, place, -1), 64)
        hot_ref[f] = jnp.concatenate([hot, hot], axis=0)


def combine_part(base_ref, loc_ref, edge_ref, m_ref, hot_ref, slot_ref, recv_ref, pt_ref, o_ref):
    me = lax.axis_index("group")
    quarter = lax.broadcasted_iota(jnp.int32, (40, 128), 1) // 32
    parts = []
    for q in range(4):
        part = None
        for s in range(4):
            shift = (32 * (s - q)) % 128
            block = m_ref[s, 0:40, :]
            block = pltpu.roll(block, shift, 1) if shift else block
            part = block if part is None else jnp.where(quarter == s, block, part)
        parts.append(part)
    incoming = jnp.concatenate(parts, axis=0) - loc_ref[...]
    projected = by_child(pt_ref, [incoming[16 * a : 16 * a + 16] for a in range(5)], recv_ref)
    values = jnp.concatenate([incoming[80:160], jnp.concatenate(projected, axis=0)], axis=1)
    hi, lo = split(values)
    spread = lax.dot_general(
        jnp.concatenate([hi, lo], axis=0),
        slot_ref[...],
        (((1,), (1,)), ((), ())),
        preferred_element_type=F32,
    )
    edge = edge_ref[...]
    before = jnp.where(me == 0, edge, m_ref[jnp.maximum(me - 1, 0), 40:160, :])
    after = jnp.where(me == 3, edge, m_ref[jnp.minimum(me + 1, 3), 40:160, :])
    lane = lax.broadcasted_iota(jnp.int32, (120, 128), 1)
    halos = []
    for packed in (before, after):
        hi = packed.astype(BF16).astype(F32)
        lo = packed - hi
        halos.append(
            jnp.concatenate(
                [
                    jnp.where(lane < 64, hi, pltpu.roll(lo, 64, 1)),
                    jnp.where(lane < 64, pltpu.roll(hi, 64, 1), lo),
                ],
                axis=0,
            ).astype(BF16)
        )
    o_ref[...] = base_ref[...]
    for f in range(6):
        third = f // 2
        far = dot(halos[f % 2][80 * third : 80 * third + 80], hot_ref[f])
        columns = slice(128 * f, 128 * f + 128)
        total = (far + spread[:80, columns] + spread[80:, columns]) * (-FACE_SCALE)
        for a in range(5):
            add_to_face(o_ref, f, a, total[16 * a : 16 * a + 16])


def local_part(
    v_ref, j_ref, visc_ref, nb_ref, g_ref, h_ref, slot_ref, recv_ref, vt_ref, it_ref, o_ref, loc_ref
):
    v = v_ref[...]
    hi, lo = split(jnp.concatenate([v[a] for a in range(5)], axis=1))
    terms = dot(vt_ref[...], jnp.concatenate([hi, lo, hi], axis=0))
    visc = visc_ref[...].reshape(1, 128)
    for a in range(5):
        total = visc * terms[192:256, 128 * a : 128 * a + 128]
        for d in range(3):
            for b in range(5):
                total = total - j_ref[a, b, d : d + 1, :] * terms[
                    64 * d : 64 * d + 64, 128 * b : 128 * b + 128
                ]
        o_ref[a] = v[a] - PSEUDO_STEP * total
    for f in range(6):
        linked, place = places(nb_ref, f)
        own = linked & (place < 128 if f % 2 else place >= 0)
        hi, lo = split(g_ref[f ^ 1])
        near = dot(jnp.concatenate([hi, lo], axis=0), one_hot(jnp.where(own, place, -1), 128))
        mask = jnp.where(nb_ref[f : f + 1, :] != -2, FACE_SCALE, 0.0)
        total = mask * h_ref[f] - FACE_SCALE * (near[:80] + near[80:])
        for a in range(5):
            add_to_face(o_ref, f, a, total[16 * a : 16 * a + 16])
    hi, lo = pick_slots(h_ref, slot_ref[...])
    picked = hi + lo
    loc_ref[...] = jnp.concatenate(
        [inter_slots(picked[:, 128:], it_ref, recv_ref), picked[:, :128]], axis=0
    )


def first_kernel(
    v_hbm, j_hbm, send_hbm, recv_hbm, it_hbm,
    g_ref, h_ref, edge_ref, m_ref, slot_ref,
    v_ref, j_ref, send_ref, recv_ref, it_ref, sems,
):
    pairs = (
        (v_hbm, v_ref), (j_hbm, j_ref), (send_hbm, send_ref), (recv_hbm, recv_ref), (it_hbm, it_ref)
    )
    copies = [pltpu.make_async_copy(a, b, sems.at[i]) for i, (a, b) in enumerate(pairs)]
    for copy in copies:
        copy.start()
    for copy in copies:
        copy.wait()
    trace_part(v_ref, j_ref, g_ref, h_ref)
    hots = slot_one_hots(send_ref, recv_ref)
    slot_ref[...] = hots
    send_part(g_ref, hots, recv_ref, it_ref, edge_ref, m_ref)


def first_local(
    v_ref, j_ref, visc_ref, nb_ref, g_ref, h_ref, slot_ref, recv_ref, vt_ref, it_ref,
    o_ref, loc_ref, hot_ref,
):
    rim_one_hots(nb_ref, hot_ref)
    local_part(
        v_ref, j_ref, visc_ref, nb_ref, g_ref, h_ref, slot_ref, recv_ref, vt_ref, it_ref, o_ref, loc_ref
    )


def middle_kernel(
    base_ref, loc_ref, edge_ref, m_ref, hot_ref, slot_ref, recv_ref, pt_ref, j_ref, it_ref,
    o_ref, g_ref, h_ref, edge2_ref, m2_ref,
):
    combine_part(base_ref, loc_ref, edge_ref, m_ref, hot_ref, slot_ref, recv_ref, pt_ref, o_ref)
    trace_part(o_ref, j_ref, g_ref, h_ref)
    send_part(g_ref, slot_ref[...], recv_ref, it_ref, edge2_ref, m2_ref)


def shape(*dims, kind=F32):
    return jax.ShapeDtypeStruct(dims, kind)


PARAMS = pltpu.CompilerParams(vmem_limit_bytes=32 * 1024 * 1024)


def call(kernel, outs, *args):
    return pl.pallas_call(kernel, out_shape=outs, compiler_params=PARAMS)(*args)


def call_from_hbm(kernel, outs, *args):
    args = [pltpu.with_memory_space_constraint(x, pltpu.HBM) for x in args]
    return pl.pallas_call(
        kernel,
        out_shape=outs,
        in_specs=[pl.BlockSpec(memory_space=pltpu.HBM)] * len(args),
        scratch_shapes=[pltpu.VMEM(x.shape, x.dtype) for x in args]
        + [pltpu.SemaphoreType.DMA((len(args),))],
        compiler_params=PARAMS,
    )(*args)


IMAGE = shape(5, 64, 128)
TRACES = shape(6, 80, 128)
EDGE = shape(120, 128)
SLOTS = shape(160, 128)
MESSAGE = shape(4, 160, 128)
SLOT_HOTS = shape(768, 256, kind=BF16)
RIM_HOTS = shape(6, 128, 128, kind=BF16)


def exchange(edge, message):
    ends = [(4 * c + 3, 4 * c + 4) for c in range(lax.axis_size("curve") - 1)]
    message = lax.all_to_all(message, "group", split_axis=0, concat_axis=0, tiled=True)
    edge = lax.ppermute(edge, AXES, ends + [(j, i) for i, j in ends])
    return edge, message


def local(tangent, jacobian, viscosity, neighbours, send_table, recv_table):
    volume_table, inter_table, project_table = (jnp.asarray(t) for t in operator_tables())
    jacobian = jnp.transpose(jacobian, (1, 2, 0, 3))
    g, h, edge, message, slots = call_from_hbm(
        first_kernel,
        (TRACES, TRACES, EDGE, MESSAGE, SLOT_HOTS),
        tangent, jacobian, send_table, recv_table, inter_table,
    )
    edge, message = exchange(edge, message)
    base, loc, hots = call(
        first_local,
        (IMAGE, SLOTS, RIM_HOTS),
        tangent, jacobian, viscosity, neighbours, g, h, slots, recv_table, volume_table, inter_table,
    )
    first, g, h, edge, message = call(
        middle_kernel,
        (IMAGE, TRACES, TRACES, EDGE, MESSAGE),
        base, loc, edge, message, hots, slots, recv_table, project_table, jacobian, inter_table,
    )
    edge, message = exchange(edge, message)
    base, loc = call(
        local_part,
        (IMAGE, SLOTS),
        first, jacobian, viscosity, neighbours, g, h, slots, recv_table, volume_table, inter_table,
    )
    second = call(
        combine_part, IMAGE, base, loc, edge, message, hots, slots, recv_table, project_table
    )
    return first, second


def solution(mesh):
    in_specs = (
        P(None, None, AXES),
        P(None, None, None, AXES),
        P(AXES),
        P(None, AXES),
        P(None, AXES),
        P(None, AXES),
    )
    out_specs = (P(None, None, AXES), P(None, None, AXES))
    return jax.shard_map(local, mesh=mesh, in_specs=in_specs, out_specs=out_specs, check_vma=False)
```

time: 50.1 us -> 47 us (0.938)
  local copies, waits for them, and re-layouts: 3.25 us -> 0.66 us
  waiting for transfers between devices: 2.66 us -> 1.56 us
    unnamed x24 -> x18, local copies, waits for them, and re-layouts: 3.25 us -> 0.66 us
    ppermute x2, waiting for transfers between devices: 2.66 us -> 1.55 us  [exchange(): edge = lax.ppermute(edge, AXES, ends + [(j, i) for i, j in ends])]
    pallas_call x7 -> x5, Pallas kernels: 6.26 us -> 6.73 us  [the longest x4 4.47 us: call(): return pl.pallas_call(kernel, out_shape=outs, compiler_params=PARAMS)(*args)]
  transfers between devices with their start and end apart: 4 -> 4, of which waited for: 2 -> 2; matrix products, arithmetic and copies ran while one was open for 0% -> 0% of each run, Pallas kernels for 2% -> 3%
where the time goes in v2:
time: 47 us; the launch traced here: 46.6 us
  starting transfers between devices  36.9 us (79%)
  Pallas kernels  6.73 us (14%)
  waiting for transfers between devices  1.56 us (3%)
  between operations  0.77 us (2%)
  local copies, waits for them, and re-layouts  0.66 us (1%)
    ppermute x2, starting transfers between devices, exchange(): edge = lax.ppermute(edge, AXES, ends + [(j, i) for i, j in ends])  28.9 us
    all_to_all x2, starting transfers between devices, exchange(): lax.all_to_all(message, 'group', split_axis=0, concat_axis=0, tiled=True)  8.02 us
    pallas_call x4, Pallas kernels, call(): return pl.pallas_call(kernel, out_shape=outs, compiler_params=PARAMS)(*args)  4.47 us
    pallas_call x1, Pallas kernels, call_from_hbm(): pl.pallas_call(kernel, out_shape=outs, in_specs=[pl.BlockSpec(memory_spac...  2.26 us
    ppermute x2, waiting for transfers between devices, exchange(): edge = lax.ppermute(edge, AXES, ends + [(j, i) for i, j in ends])  1.55 us
  transfers between devices with their start and end apart: 4, of which 2 were waited for; matrix products, arithmetic and copies ran while one was open for 0% of the time, Pallas kernels for 3%

profile of v2, /device:TPU:24, one launch (start us, length us, event | category | flops | bytes accessed | tf_op | source)
XLA Modules:
  0.0 46.6 jit_solution(18237945499538155954)
XLA Ops:
  0.6 2.3 %shard_map.104 = (f32[6,80,128]{2,1,0:T(8,128)S(1)}, f32[6,80,128]{2,1,0:T(8,128)S(1)}, f32[120,128]{1,0:T(8,128)S(1)}, f32[4,160,128]{2,1,0:T(8,128)}, bf16[768,256]{1,0:T(8,128)(2,1)S(1)}) custom-call(f32[5,64,128]{2,1,0:T(8,128)} %v_ref.1, f32[5,5,3,128]{3,2,1,0:T(4,128)} %bitcast.1, s32[3,128]{1,0:T(4,128)} %send_hbm.1, s32[4,128]{1,0:T(4,128)} %recv_ref.7, ...), custom_call_target="tpu_custom_call" | custom-call | tf_op jit(solution)/shard_map/pallas_call | solution.py:331
  2.9 0.0 copy-start
  2.9 0.0 copy-start.1
  2.9 0.0 copy-start.2
  2.9 0.0 copy-start.3
  2.9 4.4 %all-to-all-start = ((f32[4,160,128]{2,1,0:T(8,128)}), f32[4,160,128]{2,1,0:T(8,128)S(1)}, u32[]{:S(2)}, u32[]{:S(2)}) async-start(f32[4,160,128]{2,1,0:T(8,128)} %get-tuple-element.23), calls=%async_computation | async-start | bytes 655360 | tf_op jit(solution)/shard_map/all_to_all | solution.py:352
  7.4 0.0 copy-start.7
  7.4 20.5 %collective-permute-start = (f32[120,128]{1,0:T(8,128)S(1)}, f32[120,128]{1,0:T(8,128)S(1)}, u32[]{:S(2)}, u32[]{:S(2)}) collective-permute-start(f32[120,128]{1,0:T(8,128)S(1)} %get-tuple-element.22), channel_id=1, source_target_pairs={{3,4},{7,8},{11,12},{15,16},{19,20},{23,24},{27,28},{31,32},{35,36... | collective-permute-start | bytes 184328 | tf_op jit(solution)/shard_map/ppermute | solution.py:353
  27.9 0.0 copy-start.6
  27.9 0.0 copy-start.8
  27.9 0.0 copy-done
  28.0 0.0 copy-done.1
  28.0 0.0 copy-done.2
  28.0 0.0 copy-done.3
  28.0 0.0 copy-done.7
  28.0 0.6 %copy-done.6 = s32[4,128]{1,0:T(4,128)S(1)} copy-done((s32[4,128]{1,0:T(4,128)S(1)}, s32[4,128]{1,0:T(4,128)}, u32[]{:S(2)}) %copy-start.6) | copy-done | bytes 2072
  28.6 0.0 copy-done.8
  28.6 0.0 copy-start.5
  28.6 0.8 %shard_map.105 = (f32[5,64,128]{2,1,0:T(8,128)S(1)}, f32[160,128]{1,0:T(8,128)S(1)}, bf16[6,128,128]{2,1,0:T(8,128)(2,1)S(1)}) custom-call(f32[5,64,128]{2,1,0:T(8,128)S(1)} %copy-done.1, f32[5,5,3,128]{3,2,1,0:T(4,128)S(1)} %bitcast.2, f32[128]{0:T(128)S(1)} %copy-done.8, s32[6,128]{1,0:T(8,128)S(1)} %copy-done.7, ...), custom_call_target="tpu_custom_call" | custom-call | tf_op jit(solution)/shard_map/pallas_call | solution.py:326
  29.4 0.4 collective-permute-done.edge_ref
  29.8 0.0 all-to-all-done.m_ref
  29.8 0.0 copy-done.5
  29.8 1.8 %shard_map.106 = (f32[5,64,128]{2,1,0:T(8,128)}, f32[6,80,128]{2,1,0:T(8,128)S(1)}, f32[6,80,128]{2,1,0:T(8,128)S(1)}, f32[120,128]{1,0:T(8,128)S(1)}, f32[4,160,128]{2,1,0:T(8,128)}) custom-call(f32[5,64,128]{2,1,0:T(8,128)S(1)} %get-tuple-element.20.base_ref, f32[160,128]{1,0:T(8,128)S(1)} %get-tuple-element.21.loc_ref, ...), custom_call_target="tpu_custom_call" | custom-call | tf_op jit(solution)/shard_map/pallas_call | solution.py:326
  31.6 0.0 copy-start.4
  31.6 3.6 %all-to-all-start.1 = ((f32[4,160,128]{2,1,0:T(8,128)}), f32[4,160,128]{2,1,0:T(8,128)S(1)}, u32[]{:S(2)}, u32[]{:S(2)}) async-start(f32[4,160,128]{2,1,0:T(8,128)} %get-tuple-element.31), calls=%async_computation.1 | async-start | bytes 655360 | tf_op jit(solution)/shard_map/all_to_all | solution.py:352
  35.2 8.3 %collective-permute-start.1 = (f32[120,128]{1,0:T(8,128)S(1)}, f32[120,128]{1,0:T(8,128)S(1)}, u32[]{:S(2)}, u32[]{:S(2)}) collective-permute-start(f32[120,128]{1,0:T(8,128)S(1)} %get-tuple-element.30), channel_id=1, source_target_pairs={{3,4},{7,8},{11,12},{15,16},{19,20},{23,24},{27,28},{31,32},{35,36... | collective-permute-start | bytes 184328 | tf_op jit(solution)/shard_map/ppermute | solution.py:353
  43.5 0.0 copy-done.4
  43.5 0.8 %shard_map.107 = (f32[5,64,128]{2,1,0:T(8,128)S(1)}, f32[160,128]{1,0:T(8,128)S(1)}) custom-call(f32[5,64,128]{2,1,0:T(8,128)S(1)} %copy-done.4, f32[5,5,3,128]{3,2,1,0:T(4,128)S(1)} %bitcast.4, f32[128]{0:T(128)S(1)} %copy-done.8, s32[6,128]{1,0:T(8,128)S(1)} %copy-done.7, f32[6,80,128]{2,1,0:T(8,128)S(1)} %get-tuple-element.26.g_ref, ...), custom_call_target="tpu_custom_call" | custom-call | tf_op jit(solution)/shard_map/pallas_call | solution.py:326
  44.3 1.1 %collective-permute-done.1.edge_ref = f32[120,128]{1,0:T(8,128)S(1)} collective-permute-done((f32[120,128]{1,0:T(8,128)S(1)}, f32[120,128]{1,0:T(8,128)S(1)}, u32[]{:S(2)}, u32[]{:S(2)}) %collective-permute-start.1) | collective-permute-done | bytes 61472 | tf_op jit(solution)/shard_map/ppermute | solution.py:353
  45.4 0.0 all-to-all-done.1.m_ref
  45.4 1.2 %shard_map.108 = f32[5,64,128]{2,1,0:T(8,128)} custom-call(f32[5,64,128]{2,1,0:T(8,128)S(1)} %get-tuple-element.28.base_ref, f32[160,128]{1,0:T(8,128)S(1)} %get-tuple-element.29.loc_ref, f32[120,128]{1,0:T(8,128)S(1)} %collective-permute-done.1.edge_ref, f32[4,160,128]{2,1,0:T(8,128)S(1)} %all-to-all-done.1.m_ref, ...), custom_call_target="tpu_custom_call" | custom-call | tf_op jit(solution)/shard_map/pallas_call | solution.py:326
Async XLA Ops:
  2.9 25.1 %copy-start = (f32[3,5,5,128]{3,0,2,1:T(4,128)S(1)}, f32[3,5,5,128]{3,0,2,1:T(4,128)}, u32[]{:S(2)}) copy-start(f32[3,5,5,128]{3,0,2,1:T(4,128)} %param.10) | copy-start | bytes 115204
  2.9 25.0 %copy-start.1 = (f32[5,64,128]{2,1,0:T(8,128)S(1)}, f32[5,64,128]{2,1,0:T(8,128)}, u32[]{:S(2)}) copy-start(f32[5,64,128]{2,1,0:T(8,128)} %v_ref.1) | copy-start | bytes 491524
  2.9 25.0 %copy-start.2 = (bf16[256,192]{1,0:T(8,128)(2,1)S(1)}, bf16[256,192]{1,0:T(8,128)(2,1)}, u32[]{:S(2)}) copy-start(bf16[256,192]{1,0:T(8,128)(2,1)} %constant.6.clone.vt_ref) | copy-start | bytes 294916
  2.9 25.0 %copy-start.3 = (bf16[64,48]{1,0:T(8,128)(2,1)S(1)}, bf16[64,48]{1,0:T(8,128)(2,1)}, u32[]{:S(2)}) copy-start(bf16[64,48]{1,0:T(8,128)(2,1)} %constant.7.clone.it_hbm.it_ref) | copy-start | bytes 18436
  2.9 26.9 %all-to-all-start = ((f32[4,160,128]{2,1,0:T(8,128)}), f32[4,160,128]{2,1,0:T(8,128)S(1)}, u32[]{:S(2)}, u32[]{:S(2)}) async-start(f32[4,160,128]{2,1,0:T(8,128)} %get-tuple-element.23), calls=%async_computation | async-start | bytes 655360 | tf_op jit(solution)/shard_map/all_to_all | solution.py:352
  7.4 20.6 %copy-start.7 = (s32[6,128]{1,0:T(8,128)S(1)}, s32[6,128]{1,0:T(8,128)}, u32[]{:S(2)}) copy-start(s32[6,128]{1,0:T(8,128)} %nb_ref.3) | copy-start | bytes 9220
  7.4 22.4 %collective-permute-start = (f32[120,128]{1,0:T(8,128)S(1)}, f32[120,128]{1,0:T(8,128)S(1)}, u32[]{:S(2)}, u32[]{:S(2)}) collective-permute-start(f32[120,128]{1,0:T(8,128)S(1)} %get-tuple-element.22), channel_id=1, source_target_pairs={{3,4},{7,8},{11,12},{15,16},{19,20},{23,24},{27,28},{31,32},{35,36... | collective-permute-start | bytes 184328 | tf_op jit(solution)/shard_map/ppermute | solution.py:353
  27.9 0.7 %copy-start.6 = (s32[4,128]{1,0:T(4,128)S(1)}, s32[4,128]{1,0:T(4,128)}, u32[]{:S(2)}) copy-start(s32[4,128]{1,0:T(4,128)} %recv_ref.7) | copy-start | bytes 6148
  27.9 0.7 %copy-start.8 = (f32[128]{0:T(128)S(1)}, f32[128]{0:T(128)}, u32[]{:S(2)}) copy-start(f32[128]{0:T(128)} %visc_ref.3) | copy-start | bytes 1540
  28.6 1.2 %copy-start.5 = (bf16[64,48]{1,0:T(8,128)(2,1)S(1)}, bf16[64,48]{1,0:T(8,128)(2,1)}, u32[]{:S(2)}) copy-start(bf16[64,48]{1,0:T(8,128)(2,1)} %constant.8.clone.pt_ref) | copy-start | bytes 18436
  31.6 11.9 %copy-start.4 = (f32[5,64,128]{2,1,0:T(8,128)S(1)}, f32[5,64,128]{2,1,0:T(8,128)}, u32[]{:S(2)}) copy-start(f32[5,64,128]{2,1,0:T(8,128)} %get-tuple-element.15.v_ref) | copy-start | bytes 491524
  31.6 13.8 %all-to-all-start.1 = ((f32[4,160,128]{2,1,0:T(8,128)}), f32[4,160,128]{2,1,0:T(8,128)S(1)}, u32[]{:S(2)}, u32[]{:S(2)}) async-start(f32[4,160,128]{2,1,0:T(8,128)} %get-tuple-element.31), calls=%async_computation.1 | async-start | bytes 655360 | tf_op jit(solution)/shard_map/all_to_all | solution.py:352
  35.2 10.2 %collective-permute-start.1 = (f32[120,128]{1,0:T(8,128)S(1)}, f32[120,128]{1,0:T(8,128)S(1)}, u32[]{:S(2)}, u32[]{:S(2)}) collective-permute-start(f32[120,128]{1,0:T(8,128)S(1)} %get-tuple-element.30), channel_id=1, source_target_pairs={{3,4},{7,8},{11,12},{15,16},{19,20},{23,24},{27,28},{31,32},{35,36... | collective-permute-start | bytes 184328 | tf_op jit(solution)/shard_map/ppermute | solution.py:353

commit v3 on v2

--- a/solution.py
+++ b/solution.py
@@ -161,10 +161,16 @@
     return jnp.concatenate(by_child(it_ref, rows, recv_ref), axis=0)
 
 
-def send_part(g_ref, hots, recv_ref, it_ref, edge_ref, m_ref):
+def send_part(g_ref, hots, recv_ref, it_ref, edge_ref, m_ref, m_hbm, sems):
     me = lax.axis_index("group")
     up, down = rims(g_ref)
     edge_ref[...] = jnp.where(me == 0, down, up)
+    for t in range(4):
+        m_ref[t, 40:160, :] = jnp.where(me < t, up, down)
+    rim_copy = pltpu.make_async_copy(
+        m_ref.at[:, pl.ds(40, 120), :], m_hbm.at[:, pl.ds(40, 120), :], sems.at[0]
+    )
+    rim_copy.start()
     hi, lo = pick_slots(g_ref, hots)
     picked = hi + lo
     outgoing = jnp.concatenate(
@@ -179,7 +185,12 @@
             part = pltpu.roll(part, shift, 1) if shift else part
             block = part if block is None else jnp.where(quarter == q, part, block)
         m_ref[t, 0:40, :] = block
-        m_ref[t, 40:160, :] = jnp.where(me < t, up, down)
+    slot_copy = pltpu.make_async_copy(
+        m_ref.at[:, pl.ds(0, 40), :], m_hbm.at[:, pl.ds(0, 40), :], sems.at[1]
+    )
+    slot_copy.start()
+    rim_copy.wait()
+    slot_copy.wait()
 
 
 def places(nb_ref, f):
@@ -197,7 +208,20 @@
         hot_ref[f] = jnp.concatenate([hot, hot], axis=0)
 
 
-def combine_part(base_ref, loc_ref, edge_ref, m_ref, hot_ref, slot_ref, recv_ref, pt_ref, o_ref):
+def rim_pieces(packed):
+    lane = lax.broadcasted_iota(jnp.int32, (120, 128), 1)
+    hi = packed.astype(BF16).astype(F32)
+    lo = packed - hi
+    return jnp.concatenate(
+        [
+            jnp.where(lane < 64, hi, pltpu.roll(lo, 64, 1)),
+            jnp.where(lane < 64, pltpu.roll(hi, 64, 1), lo),
+        ],
+        axis=0,
+    ).astype(BF16)
+
+
+def group_part(base_ref, loc_ref, m_ref, hot_ref, slot_ref, recv_ref, pt_ref, o_ref):
     me = lax.axis_index("group")
     quarter = lax.broadcasted_iota(jnp.int32, (40, 128), 1) // 32
     parts = []
@@ -219,23 +243,9 @@
         (((1,), (1,)), ((), ())),
         preferred_element_type=F32,
     )
-    edge = edge_ref[...]
-    before = jnp.where(me == 0, edge, m_ref[jnp.maximum(me - 1, 0), 40:160, :])
-    after = jnp.where(me == 3, edge, m_ref[jnp.minimum(me + 1, 3), 40:160, :])
-    lane = lax.broadcasted_iota(jnp.int32, (120, 128), 1)
-    halos = []
-    for packed in (before, after):
-        hi = packed.astype(BF16).astype(F32)
-        lo = packed - hi
-        halos.append(
-            jnp.concatenate(
-                [
-                    jnp.where(lane < 64, hi, pltpu.roll(lo, 64, 1)),
-                    jnp.where(lane < 64, pltpu.roll(hi, 64, 1), lo),
-                ],
-                axis=0,
-            ).astype(BF16)
-        )
+    before = jnp.where(me == 0, 0.0, m_ref[jnp.maximum(me - 1, 0), 40:160, :])
+    after = jnp.where(me == 3, 0.0, m_ref[jnp.minimum(me + 1, 3), 40:160, :])
+    halos = [rim_pieces(before), rim_pieces(after)]
     o_ref[...] = base_ref[...]
     for f in range(6):
         third = f // 2
@@ -244,6 +254,21 @@
         total = (far + spread[:80, columns] + spread[80:, columns]) * (-FACE_SCALE)
         for a in range(5):
             add_to_face(o_ref, f, a, total[16 * a : 16 * a + 16])
+
+
+def edge_part(base_ref, edge_ref, hot_ref, o_ref):
+    me = lax.axis_index("group")
+    o_ref[...] = base_ref[...]
+    for end, parity in ((0, 0), (3, 1)):
+
+        @pl.when(me == end)
+        def _():
+            halo = rim_pieces(edge_ref[...])
+            for third in range(3):
+                f = 2 * third + parity
+                far = dot(halo[80 * third : 80 * third + 80], hot_ref[f]) * (-FACE_SCALE)
+                for a in range(5):
+                    add_to_face(o_ref, f, a, far[16 * a : 16 * a + 16])
 
 
 def local_part(
@@ -279,8 +304,8 @@
 
 def first_kernel(
     v_hbm, j_hbm, send_hbm, recv_hbm, it_hbm,
-    g_ref, h_ref, edge_ref, m_ref, slot_ref,
-    v_ref, j_ref, send_ref, recv_ref, it_ref, sems,
+    g_ref, h_ref, edge_ref, m_hbm, slot_ref,
+    v_ref, j_ref, send_ref, recv_ref, it_ref, m_ref, sems, m_sems,
 ):
     pairs = (
         (v_hbm, v_ref), (j_hbm, j_ref), (send_hbm, send_ref), (recv_hbm, recv_ref), (it_hbm, it_ref)
@@ -288,12 +313,13 @@
     copies = [pltpu.make_async_copy(a, b, sems.at[i]) for i, (a, b) in enumerate(pairs)]
     for copy in copies:
         copy.start()
-    for copy in copies:
+    for copy in copies[2:]:
+        copy.wait()
+    slot_ref[...] = slot_one_hots(send_ref, recv_ref)
+    for copy in copies[:2]:
         copy.wait()
     trace_part(v_ref, j_ref, g_ref, h_ref)
-    hots = slot_one_hots(send_ref, recv_ref)
-    slot_ref[...] = hots
-    send_part(g_ref, hots, recv_ref, it_ref, edge_ref, m_ref)
+    send_part(g_ref, slot_ref[...], recv_ref, it_ref, edge_ref, m_ref, m_hbm, m_sems)
 
 
 def first_local(
@@ -306,13 +332,26 @@
     )
 
 
+def second_local(
+    v_ref, j_ref, visc_ref, nb_ref, g_ref, h_ref, slot_ref, recv_ref, vt_ref, it_ref,
+    o_ref, loc_ref, v_hbm, sem,
+):
+    copy = pltpu.make_async_copy(v_ref, v_hbm, sem)
+    copy.start()
+    local_part(
+        v_ref, j_ref, visc_ref, nb_ref, g_ref, h_ref, slot_ref, recv_ref, vt_ref, it_ref, o_ref, loc_ref
+    )
+    copy.wait()
+
+
 def middle_kernel(
-    base_ref, loc_ref, edge_ref, m_ref, hot_ref, slot_ref, recv_ref, pt_ref, j_ref, it_ref,
-    o_ref, g_ref, h_ref, edge2_ref, m2_ref,
+    base_ref, edge_ref, hot_ref, slot_ref, recv_ref, j_ref, it_ref,
+    o_ref, g_ref, h_ref, edge2_ref, m_hbm,
+    m_ref, m_sems,
 ):
-    combine_part(base_ref, loc_ref, edge_ref, m_ref, hot_ref, slot_ref, recv_ref, pt_ref, o_ref)
+    edge_part(base_ref, edge_ref, hot_ref, o_ref)
     trace_part(o_ref, j_ref, g_ref, h_ref)
-    send_part(g_ref, slot_ref[...], recv_ref, it_ref, edge2_ref, m2_ref)
+    send_part(g_ref, slot_ref[...], recv_ref, it_ref, edge2_ref, m_ref, m_hbm, m_sems)
 
 
 def shape(*dims, kind=F32):
@@ -324,18 +363,6 @@
 
 def call(kernel, outs, *args):
     return pl.pallas_call(kernel, out_shape=outs, compiler_params=PARAMS)(*args)
-
-
-def call_from_hbm(kernel, outs, *args):
-    args = [pltpu.with_memory_space_constraint(x, pltpu.HBM) for x in args]
-    return pl.pallas_call(
-        kernel,
-        out_shape=outs,
-        in_specs=[pl.BlockSpec(memory_space=pltpu.HBM)] * len(args),
-        scratch_shapes=[pltpu.VMEM(x.shape, x.dtype) for x in args]
-        + [pltpu.SemaphoreType.DMA((len(args),))],
-        compiler_params=PARAMS,
-    )(*args)
 
 
 IMAGE = shape(5, 64, 128)
@@ -354,34 +381,52 @@
     return edge, message
 
 
+VMEM = pl.BlockSpec(memory_space=pltpu.VMEM)
+HBM = pl.BlockSpec(memory_space=pltpu.HBM)
+MESSAGE_SCRATCH = [pltpu.VMEM(MESSAGE.shape, F32)]
+TWO_COPIES = pltpu.SemaphoreType.DMA((2,))
+
+
 def local(tangent, jacobian, viscosity, neighbours, send_table, recv_table):
     volume_table, inter_table, project_table = (jnp.asarray(t) for t in operator_tables())
     jacobian = jnp.transpose(jacobian, (1, 2, 0, 3))
-    g, h, edge, message, slots = call_from_hbm(
+    inputs = (tangent, jacobian, send_table, recv_table, inter_table)
+    g, h, edge, message, slots = pl.pallas_call(
         first_kernel,
-        (TRACES, TRACES, EDGE, MESSAGE, SLOT_HOTS),
-        tangent, jacobian, send_table, recv_table, inter_table,
-    )
+        out_shape=(TRACES, TRACES, EDGE, MESSAGE, SLOT_HOTS),
+        in_specs=[HBM] * 5,
+        out_specs=(VMEM, VMEM, VMEM, HBM, VMEM),
+        scratch_shapes=[pltpu.VMEM(x.shape, x.dtype) for x in inputs]
+        + MESSAGE_SCRATCH
+        + [pltpu.SemaphoreType.DMA((5,)), TWO_COPIES],
+        compiler_params=PARAMS,
+    )(*(pltpu.with_memory_space_constraint(x, pltpu.HBM) for x in inputs))
     edge, message = exchange(edge, message)
     base, loc, hots = call(
         first_local,
         (IMAGE, SLOTS, RIM_HOTS),
         tangent, jacobian, viscosity, neighbours, g, h, slots, recv_table, volume_table, inter_table,
     )
-    first, g, h, edge, message = call(
+    base = call(group_part, IMAGE, base, loc, message, hots, slots, recv_table, project_table)
+    image, g, h, edge, message = pl.pallas_call(
         middle_kernel,
-        (IMAGE, TRACES, TRACES, EDGE, MESSAGE),
-        base, loc, edge, message, hots, slots, recv_table, project_table, jacobian, inter_table,
-    )
+        out_shape=(pltpu.VMEM(IMAGE.shape, F32), TRACES, TRACES, EDGE, MESSAGE),
+        in_specs=[VMEM] * 7,
+        out_specs=(VMEM, VMEM, VMEM, VMEM, HBM),
+        scratch_shapes=MESSAGE_SCRATCH + [TWO_COPIES],
+        compiler_params=PARAMS,
+    )(base, edge, hots, slots, recv_table, jacobian, inter_table)
     edge, message = exchange(edge, message)
-    base, loc = call(
-        local_part,
-        (IMAGE, SLOTS),
-        first, jacobian, viscosity, neighbours, g, h, slots, recv_table, volume_table, inter_table,
-    )
-    second = call(
-        combine_part, IMAGE, base, loc, edge, message, hots, slots, recv_table, project_table
-    )
+    base, loc, first = pl.pallas_call(
+        second_local,
+        out_shape=(IMAGE, SLOTS, IMAGE),
+        in_specs=[VMEM] * 10,
+        out_specs=(VMEM, VMEM, HBM),
+        scratch_shapes=[pltpu.SemaphoreType.DMA],
+        compiler_params=PARAMS,
+    )(image, jacobian, viscosity, neighbours, g, h, slots, recv_table, volume_table, inter_table)
+    base = call(group_part, IMAGE, base, loc, message, hots, slots, recv_table, project_table)
+    second = call(edge_part, IMAGE, base, edge, hots)
     return first, second
 
 

time: 47 us -> 46.1 us (0.981)
  waiting for transfers between devices: 1.56 us -> 0.57 us
    pallas_call x1 -> x3, Pallas kernels: 2.26 us -> 4.34 us  [the longest x1 2.14 us: local(): pl.pallas_call(first_kernel, out_shape=(TRACES, TRACES, EDGE, MESSAGE, SL...]
    pallas_call x4, Pallas kernels: 4.47 us -> 2.72 us  [call(): return pl.pallas_call(kernel, out_shape=outs, compiler_params=PARAMS)(*args)]
    ppermute x2, waiting for transfers between devices: 1.55 us -> 0.56 us  [exchange(): edge = lax.ppermute(edge, AXES, ends + [(j, i) for i, j in ends])]
  transfers between devices with their start and end apart: 4 -> 4, of which waited for: 2 -> 1; matrix products, arithmetic and copies ran while one was open for 0% -> 0% of each run, Pallas kernels for 3% -> 6%
where the time goes in v3:
time: 46.1 us; the launch traced here: 45.7 us
  starting transfers between devices  36.6 us (79%)
  Pallas kernels  7.07 us (15%)
  between operations  0.82 us (2%)
  local copies, waits for them, and re-layouts  0.65 us (1%)
  waiting for transfers between devices  0.57 us (1%)
    ppermute x2, starting transfers between devices, exchange(): edge = lax.ppermute(edge, AXES, ends + [(j, i) for i, j in ends])  28.7 us
    all_to_all x2, starting transfers between devices, exchange(): lax.all_to_all(message, 'group', split_axis=0, concat_axis=0, tiled=True)  7.9 us
    pallas_call x4, Pallas kernels, call(): return pl.pallas_call(kernel, out_shape=outs, compiler_params=PARAMS)(*args)  2.72 us
    pallas_call x1, Pallas kernels, local(): pl.pallas_call(first_kernel, out_shape=(TRACES, TRACES, EDGE, MESSAGE, SL...  2.14 us
    pallas_call x1, Pallas kernels, local(): pl.pallas_call(middle_kernel, out_shape=(pltpu.VMEM(IMAGE.shape, F32), TR...  1.42 us
  transfers between devices with their start and end apart: 4, of which 1 were waited for; matrix products, arithmetic and copies ran while one was open for 0% of the time, Pallas kernels for 6%

profile of v3, /device:TPU:24, one launch (start us, length us, event | category | flops | bytes accessed | tf_op | source)
XLA Modules:
  0.0 45.7 jit_solution(15402583385155907706)
XLA Ops:
  0.6 2.1 %shard_map.104 = (f32[6,80,128]{2,1,0:T(8,128)S(1)}, f32[6,80,128]{2,1,0:T(8,128)S(1)}, f32[120,128]{1,0:T(8,128)S(1)}, f32[4,160,128]{2,1,0:T(8,128)}, bf16[768,256]{1,0:T(8,128)(2,1)S(1)}) custom-call(f32[5,64,128]{2,1,0:T(8,128)} %v_ref.1, f32[5,5,3,128]{3,2,1,0:T(4,128)} %bitcast.1, s32[3,128]{1,0:T(4,128)} %send_hbm.1, s32[4,128]{1,0:T(4,128)} %recv_ref.9, ...), custom_call_target="tpu_custom_call" | custom-call | tf_op jit(solution)/shard_map/pallas_call | solution.py:394
  2.8 0.0 copy-start
  2.8 0.0 copy-start.1
  2.8 0.0 copy-start.2
  2.8 0.0 copy-start.3
  2.8 4.4 %all-to-all-start = ((f32[4,160,128]{2,1,0:T(8,128)}), f32[4,160,128]{2,1,0:T(8,128)S(1)}, u32[]{:S(2)}, u32[]{:S(2)}) async-start(f32[4,160,128]{2,1,0:T(8,128)} %get-tuple-element.23), calls=%async_computation | async-start | bytes 655360 | tf_op jit(solution)/shard_map/all_to_all | solution.py:379
  7.3 0.0 copy-start.6
  7.3 20.5 %collective-permute-start = (f32[120,128]{1,0:T(8,128)S(1)}, f32[120,128]{1,0:T(8,128)S(1)}, u32[]{:S(2)}, u32[]{:S(2)}) collective-permute-start(f32[120,128]{1,0:T(8,128)S(1)} %get-tuple-element.25), channel_id=1, source_target_pairs={{3,4},{7,8},{11,12},{15,16},{19,20},{23,24},{27,28},{31,32},{35,36... | collective-permute-start | bytes 184328 | tf_op jit(solution)/shard_map/ppermute | solution.py:380
  27.8 0.0 copy-start.4
  27.8 0.0 copy-start.7
  27.8 0.0 copy-done
  27.8 0.0 copy-done.1
  27.8 0.0 copy-done.2
  27.9 0.0 copy-done.3
  27.9 0.0 copy-done.6
  27.9 0.6 %copy-done.4 = s32[4,128]{1,0:T(4,128)S(1)} copy-done((s32[4,128]{1,0:T(4,128)S(1)}, s32[4,128]{1,0:T(4,128)}, u32[]{:S(2)}) %copy-start.4) | copy-done | bytes 2072
  28.5 0.0 copy-done.7
  28.5 0.0 copy-start.5
  28.5 0.8 %shard_map.105 = (f32[5,64,128]{2,1,0:T(8,128)S(1)}, f32[160,128]{1,0:T(8,128)S(1)}, bf16[6,128,128]{2,1,0:T(8,128)(2,1)S(1)}) custom-call(f32[5,64,128]{2,1,0:T(8,128)S(1)} %copy-done.1, f32[5,5,3,128]{3,2,1,0:T(4,128)S(1)} %bitcast.2, f32[128]{0:T(128)S(1)} %copy-done.7, s32[6,128]{1,0:T(8,128)S(1)} %copy-done.6, ...), custom_call_target="tpu_custom_call" | custom-call | tf_op jit(solution)/shard_map/pallas_call | solution.py:365
  29.3 0.0 all-to-all-done.m_ref
  29.3 0.0 copy-done.5
  29.3 0.5 %shard_map.106.base_ref = f32[5,64,128]{2,1,0:T(8,128)S(1)} custom-call(f32[5,64,128]{2,1,0:T(8,128)S(1)} %get-tuple-element.21.base_ref, f32[160,128]{1,0:T(8,128)S(1)} %get-tuple-element.22.loc_ref, f32[4,160,128]{2,1,0:T(8,128)S(1)} %all-to-all-done.m_ref, bf16[6,128,128]{2,1,0:T(8,128)(2,1)S(1)} %get-tuple-element.24.hot_ref, ...), custom_call_target="tpu_custom_call" | custom-call | tf_op jit(solution)/shard_map/pallas_call | solution.py:365
  29.8 0.0 collective-permute-done.edge_ref
  29.8 1.4 %shard_map.107 = (f32[5,64,128]{2,1,0:T(8,128)S(1)}, f32[6,80,128]{2,1,0:T(8,128)S(1)}, f32[6,80,128]{2,1,0:T(8,128)S(1)}, f32[120,128]{1,0:T(8,128)S(1)}, f32[4,160,128]{2,1,0:T(8,128)}) custom-call(f32[5,64,128]{2,1,0:T(8,128)S(1)} %shard_map.106.base_ref, f32[120,128]{1,0:T(8,128)S(1)} %collective-permute-done.edge_ref, ...), custom_call_target="tpu_custom_call" | custom-call | tf_op jit(solution)/shard_map/pallas_call | solution.py:411
  31.2 3.5 %all-to-all-start.1 = ((f32[4,160,128]{2,1,0:T(8,128)}), f32[4,160,128]{2,1,0:T(8,128)S(1)}, u32[]{:S(2)}, u32[]{:S(2)}) async-start(f32[4,160,128]{2,1,0:T(8,128)} %get-tuple-element.32), calls=%async_computation.1 | async-start | bytes 655360 | tf_op jit(solution)/shard_map/all_to_all | solution.py:379
  34.7 8.2 %collective-permute-start.1 = (f32[120,128]{1,0:T(8,128)S(1)}, f32[120,128]{1,0:T(8,128)S(1)}, u32[]{:S(2)}, u32[]{:S(2)}) collective-permute-start(f32[120,128]{1,0:T(8,128)S(1)} %get-tuple-element.33), channel_id=1, source_target_pairs={{3,4},{7,8},{11,12},{15,16},{19,20},{23,24},{27,28},{31,32},{35,36... | collective-permute-start | bytes 184328 | tf_op jit(solution)/shard_map/ppermute | solution.py:380
  42.9 0.8 %shard_map.108 = (f32[5,64,128]{2,1,0:T(8,128)S(1)}, f32[160,128]{1,0:T(8,128)S(1)}, f32[5,64,128]{2,1,0:T(8,128)}) custom-call(f32[5,64,128]{2,1,0:T(8,128)S(1)} %get-tuple-element.26.v_ref, f32[5,5,3,128]{3,2,1,0:T(4,128)S(1)} %bitcast.4, f32[128]{0:T(128)S(1)} %copy-done.7, s32[6,128]{1,0:T(8,128)S(1)} %copy-done.6, ...), custom_call_target="tpu_custom_call" | custom-call | tf_op jit(solution)/shard_map/pallas_call | solution.py:420
  43.7 0.0 all-to-all-done.1.m_ref
  43.7 0.5 %shard_map.109.base_ref = f32[5,64,128]{2,1,0:T(8,128)S(1)} custom-call(f32[5,64,128]{2,1,0:T(8,128)S(1)} %get-tuple-element.30.base_ref, f32[160,128]{1,0:T(8,128)S(1)} %get-tuple-element.31.loc_ref, f32[4,160,128]{2,1,0:T(8,128)S(1)} %all-to-all-done.1.m_ref, bf16[6,128,128]{2,1,0:T(8,128)(2,1)S(1)} %get-tuple-element.24.hot_ref, ...), custom_call_target="tpu_custom_call" | custom-call | tf_op jit(solution)/shard_map/pallas_call | solution.py:365
  44.3 0.6 %collective-permute-done.1.edge_ref = f32[120,128]{1,0:T(8,128)S(1)} collective-permute-done((f32[120,128]{1,0:T(8,128)S(1)}, f32[120,128]{1,0:T(8,128)S(1)}, u32[]{:S(2)}, u32[]{:S(2)}) %collective-permute-start.1) | collective-permute-done | bytes 61472 | tf_op jit(solution)/shard_map/ppermute | solution.py:380
  44.8 0.9 %shard_map.110 = f32[5,64,128]{2,1,0:T(8,128)} custom-call(f32[5,64,128]{2,1,0:T(8,128)S(1)} %shard_map.109.base_ref, f32[120,128]{1,0:T(8,128)S(1)} %collective-permute-done.1.edge_ref, bf16[6,128,128]{2,1,0:T(8,128)(2,1)S(1)} %get-tuple-element.24.hot_ref), custom_call_target="tpu_custom_call" | custom-call | tf_op jit(solution)/shard_map/pallas_call | solution.py:365
Async XLA Ops:
  2.8 25.1 %copy-start = (f32[3,5,5,128]{3,0,2,1:T(4,128)S(1)}, f32[3,5,5,128]{3,0,2,1:T(4,128)}, u32[]{:S(2)}) copy-start(f32[3,5,5,128]{3,0,2,1:T(4,128)} %param.10) | copy-start | bytes 115204
  2.8 25.0 %copy-start.1 = (f32[5,64,128]{2,1,0:T(8,128)S(1)}, f32[5,64,128]{2,1,0:T(8,128)}, u32[]{:S(2)}) copy-start(f32[5,64,128]{2,1,0:T(8,128)} %v_ref.1) | copy-start | bytes 491524
  2.8 25.0 %copy-start.2 = (bf16[256,192]{1,0:T(8,128)(2,1)S(1)}, bf16[256,192]{1,0:T(8,128)(2,1)}, u32[]{:S(2)}) copy-start(bf16[256,192]{1,0:T(8,128)(2,1)} %constant.6.clone.vt_ref) | copy-start | bytes 294916
  2.8 25.0 %copy-start.3 = (bf16[64,48]{1,0:T(8,128)(2,1)S(1)}, bf16[64,48]{1,0:T(8,128)(2,1)}, u32[]{:S(2)}) copy-start(bf16[64,48]{1,0:T(8,128)(2,1)} %constant.7.clone.it_hbm.it_ref) | copy-start | bytes 18436
  2.8 26.4 %all-to-all-start = ((f32[4,160,128]{2,1,0:T(8,128)}), f32[4,160,128]{2,1,0:T(8,128)S(1)}, u32[]{:S(2)}, u32[]{:S(2)}) async-start(f32[4,160,128]{2,1,0:T(8,128)} %get-tuple-element.23), calls=%async_computation | async-start | bytes 655360 | tf_op jit(solution)/shard_map/all_to_all | solution.py:379
  7.3 20.6 %copy-start.6 = (s32[6,128]{1,0:T(8,128)S(1)}, s32[6,128]{1,0:T(8,128)}, u32[]{:S(2)}) copy-start(s32[6,128]{1,0:T(8,128)} %nb_ref.3) | copy-start | bytes 9220
  7.3 22.5 %collective-permute-start = (f32[120,128]{1,0:T(8,128)S(1)}, f32[120,128]{1,0:T(8,128)S(1)}, u32[]{:S(2)}, u32[]{:S(2)}) collective-permute-start(f32[120,128]{1,0:T(8,128)S(1)} %get-tuple-element.25), channel_id=1, source_target_pairs={{3,4},{7,8},{11,12},{15,16},{19,20},{23,24},{27,28},{31,32},{35,36... | collective-permute-start | bytes 184328 | tf_op jit(solution)/shard_map/ppermute | solution.py:380
  27.8 0.7 %copy-start.4 = (s32[4,128]{1,0:T(4,128)S(1)}, s32[4,128]{1,0:T(4,128)}, u32[]{:S(2)}) copy-start(s32[4,128]{1,0:T(4,128)} %recv_ref.9) | copy-start | bytes 6148
  27.8 0.7 %copy-start.7 = (f32[128]{0:T(128)S(1)}, f32[128]{0:T(128)}, u32[]{:S(2)}) copy-start(f32[128]{0:T(128)} %visc_ref.3) | copy-start | bytes 1540
  28.5 0.8 %copy-start.5 = (bf16[64,48]{1,0:T(8,128)(2,1)S(1)}, bf16[64,48]{1,0:T(8,128)(2,1)}, u32[]{:S(2)}) copy-start(bf16[64,48]{1,0:T(8,128)(2,1)} %constant.8.clone.pt_ref) | copy-start | bytes 18436
  31.2 12.5 %all-to-all-start.1 = ((f32[4,160,128]{2,1,0:T(8,128)}), f32[4,160,128]{2,1,0:T(8,128)S(1)}, u32[]{:S(2)}, u32[]{:S(2)}) async-start(f32[4,160,128]{2,1,0:T(8,128)} %get-tuple-element.32), calls=%async_computation.1 | async-start | bytes 655360 | tf_op jit(solution)/shard_map/all_to_all | solution.py:379
  34.7 10.1 %collective-permute-start.1 = (f32[120,128]{1,0:T(8,128)S(1)}, f32[120,128]{1,0:T(8,128)S(1)}, u32[]{:S(2)}, u32[]{:S(2)}) collective-permute-start(f32[120,128]{1,0:T(8,128)S(1)} %get-tuple-element.33), channel_id=1, source_target_pairs={{3,4},{7,8},{11,12},{15,16},{19,20},{23,24},{27,28},{31,32},{35,36... | collective-permute-start | bytes 184328 | tf_op jit(solution)/shard_map/ppermute | solution.py:380

commit v4 on v3

--- a/solution.py
+++ b/solution.py
@@ -271,9 +271,15 @@
                     add_to_face(o_ref, f, a, far[16 * a : 16 * a + 16])
 
 
-def local_part(
-    v_ref, j_ref, visc_ref, nb_ref, g_ref, h_ref, slot_ref, recv_ref, vt_ref, it_ref, o_ref, loc_ref
-):
+def slot_terms(h_ref, slot_ref, recv_ref, it_ref, loc_ref):
+    hi, lo = pick_slots(h_ref, slot_ref[...])
+    picked = hi + lo
+    loc_ref[...] = jnp.concatenate(
+        [inter_slots(picked[:, 128:], it_ref, recv_ref), picked[:, :128]], axis=0
+    )
+
+
+def local_part(v_ref, j_ref, visc_ref, nb_ref, g_ref, h_ref, vt_ref, o_ref):
     v = v_ref[...]
     hi, lo = split(jnp.concatenate([v[a] for a in range(5)], axis=1))
     terms = dot(vt_ref[...], jnp.concatenate([hi, lo, hi], axis=0))
@@ -295,17 +301,12 @@
         total = mask * h_ref[f] - FACE_SCALE * (near[:80] + near[80:])
         for a in range(5):
             add_to_face(o_ref, f, a, total[16 * a : 16 * a + 16])
-    hi, lo = pick_slots(h_ref, slot_ref[...])
-    picked = hi + lo
-    loc_ref[...] = jnp.concatenate(
-        [inter_slots(picked[:, 128:], it_ref, recv_ref), picked[:, :128]], axis=0
-    )
 
 
 def first_kernel(
     v_hbm, j_hbm, send_hbm, recv_hbm, it_hbm,
-    g_ref, h_ref, edge_ref, m_hbm, slot_ref,
-    v_ref, j_ref, send_ref, recv_ref, it_ref, m_ref, sems, m_sems,
+    g_ref, h_ref, edge_ref, m_hbm, slot_ref, v_ref, j_ref, recv_ref, it_ref,
+    send_ref, m_ref, sems, m_sems,
 ):
     pairs = (
         (v_hbm, v_ref), (j_hbm, j_ref), (send_hbm, send_ref), (recv_hbm, recv_ref), (it_hbm, it_ref)
@@ -323,13 +324,18 @@
 
 
 def first_local(
-    v_ref, j_ref, visc_ref, nb_ref, g_ref, h_ref, slot_ref, recv_ref, vt_ref, it_ref,
-    o_ref, loc_ref, hot_ref,
+    v_ref, j_ref, g_ref, h_ref, slot_ref, recv_ref, it_ref, visc_hbm, nb_hbm, vt_hbm, pt_hbm,
+    o_ref, loc_ref, hot_ref, visc_ref, nb_ref, vt_ref, pt_ref, sems,
 ):
+    pairs = ((visc_hbm, visc_ref), (nb_hbm, nb_ref), (vt_hbm, vt_ref), (pt_hbm, pt_ref))
+    copies = [pltpu.make_async_copy(a, b, sems.at[i]) for i, (a, b) in enumerate(pairs)]
+    for copy in copies:
+        copy.start()
+    slot_terms(h_ref, slot_ref, recv_ref, it_ref, loc_ref)
+    for copy in copies:
+        copy.wait()
     rim_one_hots(nb_ref, hot_ref)
-    local_part(
-        v_ref, j_ref, visc_ref, nb_ref, g_ref, h_ref, slot_ref, recv_ref, vt_ref, it_ref, o_ref, loc_ref
-    )
+    local_part(v_ref, j_ref, visc_ref, nb_ref, g_ref, h_ref, vt_ref, o_ref)
 
 
 def second_local(
@@ -338,9 +344,8 @@
 ):
     copy = pltpu.make_async_copy(v_ref, v_hbm, sem)
     copy.start()
-    local_part(
-        v_ref, j_ref, visc_ref, nb_ref, g_ref, h_ref, slot_ref, recv_ref, vt_ref, it_ref, o_ref, loc_ref
-    )
+    slot_terms(h_ref, slot_ref, recv_ref, it_ref, loc_ref)
+    local_part(v_ref, j_ref, visc_ref, nb_ref, g_ref, h_ref, vt_ref, o_ref)
     copy.wait()
 
 
@@ -387,26 +392,35 @@
 TWO_COPIES = pltpu.SemaphoreType.DMA((2,))
 
 
+def in_hbm(*args):
+    return [pltpu.with_memory_space_constraint(x, pltpu.HBM) for x in args]
+
+
 def local(tangent, jacobian, viscosity, neighbours, send_table, recv_table):
     volume_table, inter_table, project_table = (jnp.asarray(t) for t in operator_tables())
     jacobian = jnp.transpose(jacobian, (1, 2, 0, 3))
     inputs = (tangent, jacobian, send_table, recv_table, inter_table)
-    g, h, edge, message, slots = pl.pallas_call(
+    g, h, edge, message, slots, tangent, jacobian, recv_table, inter_table = pl.pallas_call(
         first_kernel,
-        out_shape=(TRACES, TRACES, EDGE, MESSAGE, SLOT_HOTS),
+        out_shape=(TRACES, TRACES, EDGE, MESSAGE, SLOT_HOTS)
+        + tuple(pltpu.VMEM(inputs[i].shape, inputs[i].dtype) for i in (0, 1, 3, 4)),
         in_specs=[HBM] * 5,
-        out_specs=(VMEM, VMEM, VMEM, HBM, VMEM),
-        scratch_shapes=[pltpu.VMEM(x.shape, x.dtype) for x in inputs]
+        out_specs=(VMEM, VMEM, VMEM, HBM) + (VMEM,) * 5,
+        scratch_shapes=[pltpu.VMEM(send_table.shape, send_table.dtype)]
         + MESSAGE_SCRATCH
         + [pltpu.SemaphoreType.DMA((5,)), TWO_COPIES],
         compiler_params=PARAMS,
-    )(*(pltpu.with_memory_space_constraint(x, pltpu.HBM) for x in inputs))
+    )(*in_hbm(*inputs))
     edge, message = exchange(edge, message)
-    base, loc, hots = call(
+    inputs = (viscosity, neighbours, volume_table, project_table)
+    base, loc, hots, viscosity, neighbours, volume_table, project_table = pl.pallas_call(
         first_local,
-        (IMAGE, SLOTS, RIM_HOTS),
-        tangent, jacobian, viscosity, neighbours, g, h, slots, recv_table, volume_table, inter_table,
-    )
+        out_shape=(IMAGE, SLOTS, RIM_HOTS) + tuple(pltpu.VMEM(x.shape, x.dtype) for x in inputs),
+        in_specs=[VMEM] * 7 + [HBM] * 4,
+        out_specs=(VMEM,) * 7,
+        scratch_shapes=[pltpu.SemaphoreType.DMA((4,))],
+        compiler_params=PARAMS,
+    )(tangent, jacobian, g, h, slots, recv_table, inter_table, *in_hbm(*inputs))
     base = call(group_part, IMAGE, base, loc, message, hots, slots, recv_table, project_table)
     image, g, h, edge, message = pl.pallas_call(
         middle_kernel,

time: 46.1 us -> 45.7 us (level)
  Pallas kernels: 7.07 us -> 7.78 us
  local copies, waits for them, and re-layouts: 0.65 us -> 0 us
    pallas_call x0 -> x1, Pallas kernels: none -> 1.48 us  [local(): pl.pallas_call(first_local, out_shape=(IMAGE, SLOTS, RIM_HOTS) + tuple((p...]
    pallas_call x4 -> x3, Pallas kernels: 2.72 us -> 1.97 us  [call(): return pl.pallas_call(kernel, out_shape=outs, compiler_params=PARAMS)(*args)]
    unnamed x16 -> x0, local copies, waits for them, and re-layouts: 0.65 us -> none
  transfers between devices with their start and end apart: 4 -> 4, of which waited for: 1 -> 1; matrix products, arithmetic and copies ran while one was open for 0% -> 0% of each run, Pallas kernels for 6% -> 7%
where the time goes in v4:
time: 45.7 us; the launch traced here: 45.4 us
  starting transfers between devices  36.3 us (79%)
  Pallas kernels  7.78 us (17%)
  between operations  0.72 us (2%)
  waiting for transfers between devices  0.56 us (1%)
    ppermute x2, starting transfers between devices, exchange(): edge = lax.ppermute(edge, AXES, ends + [(j, i) for i, j in ends])  28.6 us
    all_to_all x2, starting transfers between devices, exchange(): lax.all_to_all(message, 'group', split_axis=0, concat_axis=0, tiled=True)  7.77 us
    pallas_call x1, Pallas kernels, local(): pl.pallas_call(first_kernel, out_shape=(TRACES, TRACES, EDGE, MESSAGE, SL...  2.13 us
    pallas_call x3, Pallas kernels, call(): return pl.pallas_call(kernel, out_shape=outs, compiler_params=PARAMS)(*args)  1.97 us
    pallas_call x1, Pallas kernels, local(): pl.pallas_call(first_local, out_shape=(IMAGE, SLOTS, RIM_HOTS) + tuple((p...  1.48 us
    pallas_call x1, Pallas kernels, local(): pl.pallas_call(middle_kernel, out_shape=(pltpu.VMEM(IMAGE.shape, F32), TR...  1.41 us
  transfers between devices with their start and end apart: 4, of which 1 were waited for; matrix products, arithmetic and copies ran while one was open for 0% of the time, Pallas kernels for 7%

profile of v4, /device:TPU:24, one launch (start us, length us, event | category | flops | bytes accessed | tf_op | source)
XLA Modules:
  0.0 45.4 jit_solution(12575403432821741190)
XLA Ops:
  0.6 2.1 %shard_map.104 = (f32[6,80,128]{2,1,0:T(8,128)S(1)}, f32[6,80,128]{2,1,0:T(8,128)S(1)}, f32[120,128]{1,0:T(8,128)S(1)}, f32[4,160,128]{2,1,0:T(8,128)}, bf16[768...) custom-call(f32[5,64,128]{2,1,0:T(8,128)} %v_hbm.1, ...), custom_call_target="tpu_custom_call" | custom-call | tf_op jit(solution)/shard_map/pallas_call | solution.py:403
  2.8 4.3 %all-to-all-start = ((f32[4,160,128]{2,1,0:T(8,128)}), f32[4,160,128]{2,1,0:T(8,128)S(1)}, u32[]{:S(2)}, u32[]{:S(2)}) async-start(f32[4,160,128]{2,1,0:T(8,128)} %get-tuple-element.35), calls=%async_computation | async-start | bytes 655360 | tf_op jit(solution)/shard_map/all_to_all | solution.py:384
  7.1 20.4 %collective-permute-start = (f32[120,128]{1,0:T(8,128)S(1)}, f32[120,128]{1,0:T(8,128)S(1)}, u32[]{:S(2)}, u32[]{:S(2)}) collective-permute-start(f32[120,128]{1,0:T(8,128)S(1)} %get-tuple-element.38), channel_id=1, source_target_pairs={{3,4},{7,8},{11,12},{15,16},{19,20},{23,24},{27,28},{31,32},{35,36... | collective-permute-start | bytes 184328 | tf_op jit(solution)/shard_map/ppermute | solution.py:385
  27.5 1.5 %shard_map.105 = (f32[5,64,128]{2,1,0:T(8,128)S(1)}, f32[160,128]{1,0:T(8,128)S(1)}, bf16[6,128,128]{2,1,0:T(8,128)(2,1)S(1)}, f32[128]{0:T(128)S(1)}, s32[6,128...) custom-call(f32[5,64,128]{2,1,0:T(8,128)S(1)} %get-tuple-element.26.v_ref, ...), custom_call_target="tpu_custom_call" | custom-call | tf_op jit(solution)/shard_map/pallas_call | solution.py:416
  29.0 0.0 all-to-all-done.m_ref
  29.0 0.5 %shard_map.106.base_ref = f32[5,64,128]{2,1,0:T(8,128)S(1)} custom-call(f32[5,64,128]{2,1,0:T(8,128)S(1)} %get-tuple-element.33.base_ref, f32[160,128]{1,0:T(8,128)S(1)} %get-tuple-element.34.loc_ref, f32[4,160,128]{2,1,0:T(8,128)S(1)} %all-to-all-done.m_ref, bf16[6,128,128]{2,1,0:T(8,128)(2,1)S(1)} %get-tuple-element.36.hot_ref, ...), custom_call_target="tpu_custom_call" | custom-call | tf_op jit(solution)/shard_map/pallas_call | solution.py:370
  29.5 0.0 collective-permute-done.edge_ref
  29.5 1.4 %shard_map.107 = (f32[5,64,128]{2,1,0:T(8,128)S(1)}, f32[6,80,128]{2,1,0:T(8,128)S(1)}, f32[6,80,128]{2,1,0:T(8,128)S(1)}, f32[120,128]{1,0:T(8,128)S(1)}, f32[4,160,128]{2,1,0:T(8,128)}) custom-call(f32[5,64,128]{2,1,0:T(8,128)S(1)} %shard_map.106.base_ref, f32[120,128]{1,0:T(8,128)S(1)} %collective-permute-done.edge_ref, ...), custom_call_target="tpu_custom_call" | custom-call | tf_op jit(solution)/shard_map/pallas_call | solution.py:425
  30.9 3.5 %all-to-all-start.1 = ((f32[4,160,128]{2,1,0:T(8,128)}), f32[4,160,128]{2,1,0:T(8,128)S(1)}, u32[]{:S(2)}, u32[]{:S(2)}) async-start(f32[4,160,128]{2,1,0:T(8,128)} %get-tuple-element.48), calls=%async_computation.1 | async-start | bytes 655360 | tf_op jit(solution)/shard_map/all_to_all | solution.py:384
  34.4 8.2 %collective-permute-start.1 = (f32[120,128]{1,0:T(8,128)S(1)}, f32[120,128]{1,0:T(8,128)S(1)}, u32[]{:S(2)}, u32[]{:S(2)}) collective-permute-start(f32[120,128]{1,0:T(8,128)S(1)} %get-tuple-element.49), channel_id=1, source_target_pairs={{3,4},{7,8},{11,12},{15,16},{19,20},{23,24},{27,28},{31,32},{35,36... | collective-permute-start | bytes 184328 | tf_op jit(solution)/shard_map/ppermute | solution.py:385
  42.6 0.8 %shard_map.108 = (f32[5,64,128]{2,1,0:T(8,128)S(1)}, f32[160,128]{1,0:T(8,128)S(1)}, f32[5,64,128]{2,1,0:T(8,128)}) custom-call(f32[5,64,128]{2,1,0:T(8,128)S(1)} %get-tuple-element.39.v_ref, f32[5,5,3,128]{3,2,1,0:T(4,128)S(1)} %get-tuple-element.27.j_ref, f32[128]{0:T(128)S(1)} %get-tuple-element.40.visc_ref, s32[6,128]{1,0:T(8,128)S(1)} %get-tuple-element.41.nb_ref, ...), custom_call_target="tpu_custom_call" | custom-call | tf_op jit(solution)/shard_map/pallas_call | solution.py:434
  43.4 0.0 all-to-all-done.1.m_ref
  43.4 0.5 %shard_map.109.base_ref = f32[5,64,128]{2,1,0:T(8,128)S(1)} custom-call(f32[5,64,128]{2,1,0:T(8,128)S(1)} %get-tuple-element.46.base_ref, f32[160,128]{1,0:T(8,128)S(1)} %get-tuple-element.47.loc_ref, f32[4,160,128]{2,1,0:T(8,128)S(1)} %all-to-all-done.1.m_ref, bf16[6,128,128]{2,1,0:T(8,128)(2,1)S(1)} %get-tuple-element.36.hot_ref, ...), custom_call_target="tpu_custom_call" | custom-call | tf_op jit(solution)/shard_map/pallas_call | solution.py:370
  43.9 0.6 %collective-permute-done.1.edge_ref = f32[120,128]{1,0:T(8,128)S(1)} collective-permute-done((f32[120,128]{1,0:T(8,128)S(1)}, f32[120,128]{1,0:T(8,128)S(1)}, u32[]{:S(2)}, u32[]{:S(2)}) %collective-permute-start.1) | collective-permute-done | bytes 61472 | tf_op jit(solution)/shard_map/ppermute | solution.py:385
  44.5 0.9 %shard_map.110 = f32[5,64,128]{2,1,0:T(8,128)} custom-call(f32[5,64,128]{2,1,0:T(8,128)S(1)} %shard_map.109.base_ref, f32[120,128]{1,0:T(8,128)S(1)} %collective-permute-done.1.edge_ref, bf16[6,128,128]{2,1,0:T(8,128)(2,1)S(1)} %get-tuple-element.36.hot_ref), custom_call_target="tpu_custom_call" | custom-call | tf_op jit(solution)/shard_map/pallas_call | solution.py:370
Async XLA Ops:
  2.8 26.2 %all-to-all-start = ((f32[4,160,128]{2,1,0:T(8,128)}), f32[4,160,128]{2,1,0:T(8,128)S(1)}, u32[]{:S(2)}, u32[]{:S(2)}) async-start(f32[4,160,128]{2,1,0:T(8,128)} %get-tuple-element.35), calls=%async_computation | async-start | bytes 655360 | tf_op jit(solution)/shard_map/all_to_all | solution.py:384
  7.1 22.4 %collective-permute-start = (f32[120,128]{1,0:T(8,128)S(1)}, f32[120,128]{1,0:T(8,128)S(1)}, u32[]{:S(2)}, u32[]{:S(2)}) collective-permute-start(f32[120,128]{1,0:T(8,128)S(1)} %get-tuple-element.38), channel_id=1, source_target_pairs={{3,4},{7,8},{11,12},{15,16},{19,20},{23,24},{27,28},{31,32},{35,36... | collective-permute-start | bytes 184328 | tf_op jit(solution)/shard_map/ppermute | solution.py:385
  30.9 12.5 %all-to-all-start.1 = ((f32[4,160,128]{2,1,0:T(8,128)}), f32[4,160,128]{2,1,0:T(8,128)S(1)}, u32[]{:S(2)}, u32[]{:S(2)}) async-start(f32[4,160,128]{2,1,0:T(8,128)} %get-tuple-element.48), calls=%async_computation.1 | async-start | bytes 655360 | tf_op jit(solution)/shard_map/all_to_all | solution.py:384
  34.4 10.1 %collective-permute-start.1 = (f32[120,128]{1,0:T(8,128)S(1)}, f32[120,128]{1,0:T(8,128)S(1)}, u32[]{:S(2)}, u32[]{:S(2)}) collective-permute-start(f32[120,128]{1,0:T(8,128)S(1)} %get-tuple-element.49), channel_id=1, source_target_pairs={{3,4},{7,8},{11,12},{15,16},{19,20},{23,24},{27,28},{31,32},{35,36... | collective-permute-start | bytes 184328 | tf_op jit(solution)/shard_map/ppermute | solution.py:385

commit v5 on v4

--- a/solution.py
+++ b/solution.py
@@ -127,9 +127,9 @@
         o_ref[a, 48 * s : 48 * s + 16, :] += values
 
 
-def rims(g_ref):
-    odd = jnp.concatenate([g_ref[1], g_ref[3], g_ref[5]], axis=0)
-    even = jnp.concatenate([g_ref[0], g_ref[2], g_ref[4]], axis=0)
+def rims(g):
+    odd = jnp.concatenate([g[1], g[3], g[5]], axis=0)
+    even = jnp.concatenate([g[0], g[2], g[4]], axis=0)
     lane = lax.broadcasted_iota(jnp.int32, (120, 128), 1)
     up = jnp.where(lane < 64, pltpu.roll(odd[:120], 64, 1), odd[120:])
     down = jnp.where(lane < 64, even[:120], pltpu.roll(even[120:], 64, 1))
@@ -137,21 +137,27 @@
 
 
 def trace_part(v_ref, j_ref, g_ref, h_ref):
+    values = []
     for f in range(6):
         d = f // 2
         w = [face_values(v_ref, f, b) for b in range(5)]
+        parts = []
         for a in range(5):
             q = j_ref[a, 0, d : d + 1, :] * w[0]
             for b in range(1, 5):
                 q = q + j_ref[a, b, d : d + 1, :] * w[b]
             rows = slice(16 * a, 16 * a + 16)
-            plus, minus = (g_ref, h_ref) if f % 2 else (h_ref, g_ref)
-            plus[f, rows, :] = w[a] + q
-            minus[f, rows, :] = w[a] - q
-
-
-def pick_slots(t_ref, hots):
-    hi, lo = split(jnp.concatenate([t_ref[f] for f in range(6)], axis=1))
+            plus, minus = w[a] + q, w[a] - q
+            g, h = (plus, minus) if f % 2 else (minus, plus)
+            g_ref[f, rows, :] = g
+            h_ref[f, rows, :] = h
+            parts.append(g)
+        values.append(jnp.concatenate(parts, axis=0))
+    return values
+
+
+def pick_slots(t, hots):
+    hi, lo = split(jnp.concatenate([t[f] for f in range(6)], axis=1))
     picked = dot(jnp.concatenate([hi, lo], axis=0), hots)
     return picked[:80], picked[80:]
 
@@ -161,17 +167,19 @@
     return jnp.concatenate(by_child(it_ref, rows, recv_ref), axis=0)
 
 
-def send_part(g_ref, hots, recv_ref, it_ref, edge_ref, m_ref, m_hbm, sems):
+def send_part(g, hots, recv_ref, it_ref, edge_ref, slots_ref, rims_ref, m_hbm, sems):
     me = lax.axis_index("group")
-    up, down = rims(g_ref)
+    up, down = rims(g)
     edge_ref[...] = jnp.where(me == 0, down, up)
-    for t in range(4):
-        m_ref[t, 40:160, :] = jnp.where(me < t, up, down)
-    rim_copy = pltpu.make_async_copy(
-        m_ref.at[:, pl.ds(40, 120), :], m_hbm.at[:, pl.ds(40, 120), :], sems.at[0]
-    )
-    rim_copy.start()
-    hi, lo = pick_slots(g_ref, hots)
+    rims_ref[0] = down
+    rims_ref[1] = up
+    copies = [
+        pltpu.make_async_copy(rims_ref.at[i], m_hbm.at[t, pl.ds(40, 120), :], sems.at[i])
+        for i, t in enumerate((jnp.maximum(me - 1, 0), jnp.minimum(me + 1, 3)))
+    ]
+    for copy in copies:
+        copy.start()
+    hi, lo = pick_slots(g, hots)
     picked = hi + lo
     outgoing = jnp.concatenate(
         [picked[:, :128], inter_slots(picked[:, 128:], it_ref, recv_ref)], axis=0
@@ -184,13 +192,12 @@
             shift = (32 * (q - t)) % 128
             part = pltpu.roll(part, shift, 1) if shift else part
             block = part if block is None else jnp.where(quarter == q, part, block)
-        m_ref[t, 0:40, :] = block
-    slot_copy = pltpu.make_async_copy(
-        m_ref.at[:, pl.ds(0, 40), :], m_hbm.at[:, pl.ds(0, 40), :], sems.at[1]
-    )
-    slot_copy.start()
-    rim_copy.wait()
-    slot_copy.wait()
+        slots_ref[t] = block
+    copies.append(
+        pltpu.make_async_copy(slots_ref, m_hbm.at[:, pl.ds(0, 40), :], sems.at[2])
+    )
+    copies[-1].start()
+    return copies
 
 
 def places(nb_ref, f):
@@ -256,14 +263,13 @@
             add_to_face(o_ref, f, a, total[16 * a : 16 * a + 16])
 
 
-def edge_part(base_ref, edge_ref, hot_ref, o_ref):
+def edge_part(edge_ref, hot_ref, o_ref):
     me = lax.axis_index("group")
-    o_ref[...] = base_ref[...]
     for end, parity in ((0, 0), (3, 1)):
 
         @pl.when(me == end)
         def _():
-            halo = rim_pieces(edge_ref[...])
+            halo = rim_pieces(edge_ref[120 * parity : 120 * parity + 120, :])
             for third in range(3):
                 f = 2 * third + parity
                 far = dot(halo[80 * third : 80 * third + 80], hot_ref[f]) * (-FACE_SCALE)
@@ -304,59 +310,56 @@
 
 
 def first_kernel(
-    v_hbm, j_hbm, send_hbm, recv_hbm, it_hbm,
-    g_ref, h_ref, edge_ref, m_hbm, slot_ref, v_ref, j_ref, recv_ref, it_ref,
-    send_ref, m_ref, sems, m_sems,
+    v_hbm, j_hbm, send_hbm, recv_hbm, it_hbm, visc_hbm, nb_hbm, vt_hbm, pt_hbm,
+    edge_ref, m_hbm, slot_ref, base_ref, loc_ref, hot_ref,
+    j_ref, recv_ref, it_ref, visc_ref, nb_ref, vt_ref, pt_ref,
+    v_ref, send_ref, g_ref, h_ref, slots_ref, rims_ref, m_sems, sems,
 ):
     pairs = (
-        (v_hbm, v_ref), (j_hbm, j_ref), (send_hbm, send_ref), (recv_hbm, recv_ref), (it_hbm, it_ref)
+        (v_hbm, v_ref), (j_hbm, j_ref), (send_hbm, send_ref), (recv_hbm, recv_ref), (it_hbm, it_ref),
+        (visc_hbm, visc_ref), (nb_hbm, nb_ref), (vt_hbm, vt_ref), (pt_hbm, pt_ref),
     )
     copies = [pltpu.make_async_copy(a, b, sems.at[i]) for i, (a, b) in enumerate(pairs)]
     for copy in copies:
         copy.start()
-    for copy in copies[2:]:
+    for copy in copies[2:5]:
         copy.wait()
     slot_ref[...] = slot_one_hots(send_ref, recv_ref)
     for copy in copies[:2]:
         copy.wait()
-    trace_part(v_ref, j_ref, g_ref, h_ref)
-    send_part(g_ref, slot_ref[...], recv_ref, it_ref, edge_ref, m_ref, m_hbm, m_sems)
-
-
-def first_local(
-    v_ref, j_ref, g_ref, h_ref, slot_ref, recv_ref, it_ref, visc_hbm, nb_hbm, vt_hbm, pt_hbm,
-    o_ref, loc_ref, hot_ref, visc_ref, nb_ref, vt_ref, pt_ref, sems,
-):
-    pairs = ((visc_hbm, visc_ref), (nb_hbm, nb_ref), (vt_hbm, vt_ref), (pt_hbm, pt_ref))
-    copies = [pltpu.make_async_copy(a, b, sems.at[i]) for i, (a, b) in enumerate(pairs)]
-    for copy in copies:
-        copy.start()
-    slot_terms(h_ref, slot_ref, recv_ref, it_ref, loc_ref)
-    for copy in copies:
+    g = trace_part(v_ref, j_ref, g_ref, h_ref)
+    sent = send_part(g, slot_ref[...], recv_ref, it_ref, edge_ref, slots_ref, rims_ref, m_hbm, m_sems)
+    for copy in copies[5:]:
         copy.wait()
     rim_one_hots(nb_ref, hot_ref)
-    local_part(v_ref, j_ref, visc_ref, nb_ref, g_ref, h_ref, vt_ref, o_ref)
-
-
-def second_local(
-    v_ref, j_ref, visc_ref, nb_ref, g_ref, h_ref, slot_ref, recv_ref, vt_ref, it_ref,
-    o_ref, loc_ref, v_hbm, sem,
+    slot_terms(h_ref, slot_ref, recv_ref, it_ref, loc_ref)
+    local_part(v_ref, j_ref, visc_ref, nb_ref, g_ref, h_ref, vt_ref, base_ref)
+    for copy in sent:
+        copy.wait()
+
+
+def middle_kernel(
+    base_ref, loc_ref, m_ref, edge_ref, hot_ref, slot_ref,
+    j_ref, recv_ref, it_ref, visc_ref, nb_ref, vt_ref, pt_ref,
+    v_hbm, edge2_ref, m_hbm, base2_ref, loc2_ref,
+    v_ref, g_ref, h_ref, slots_ref, rims_ref, m_sems, sem,
 ):
-    copy = pltpu.make_async_copy(v_ref, v_hbm, sem)
-    copy.start()
-    slot_terms(h_ref, slot_ref, recv_ref, it_ref, loc_ref)
-    local_part(v_ref, j_ref, visc_ref, nb_ref, g_ref, h_ref, vt_ref, o_ref)
-    copy.wait()
-
-
-def middle_kernel(
-    base_ref, edge_ref, hot_ref, slot_ref, recv_ref, j_ref, it_ref,
-    o_ref, g_ref, h_ref, edge2_ref, m_hbm,
-    m_ref, m_sems,
-):
-    edge_part(base_ref, edge_ref, hot_ref, o_ref)
-    trace_part(o_ref, j_ref, g_ref, h_ref)
-    send_part(g_ref, slot_ref[...], recv_ref, it_ref, edge2_ref, m_ref, m_hbm, m_sems)
+    group_part(base_ref, loc_ref, m_ref, hot_ref, slot_ref, recv_ref, pt_ref, v_ref)
+    edge_part(edge_ref, hot_ref, v_ref)
+    g = trace_part(v_ref, j_ref, g_ref, h_ref)
+    sent = send_part(g, slot_ref[...], recv_ref, it_ref, edge2_ref, slots_ref, rims_ref, m_hbm, m_sems)
+    image = pltpu.make_async_copy(v_ref, v_hbm, sem)
+    image.start()
+    slot_terms(h_ref, slot_ref, recv_ref, it_ref, loc2_ref)
+    local_part(v_ref, j_ref, visc_ref, nb_ref, g_ref, h_ref, vt_ref, base2_ref)
+    for copy in sent:
+        copy.wait()
+    image.wait()
+
+
+def last_kernel(base_ref, loc_ref, m_ref, edge_ref, hot_ref, slot_ref, recv_ref, pt_ref, o_ref):
+    group_part(base_ref, loc_ref, m_ref, hot_ref, slot_ref, recv_ref, pt_ref, o_ref)
+    edge_part(edge_ref, hot_ref, o_ref)
 
 
 def shape(*dims, kind=F32):
@@ -366,12 +369,7 @@
 PARAMS = pltpu.CompilerParams(vmem_limit_bytes=32 * 1024 * 1024)
 
 
-def call(kernel, outs, *args):
-    return pl.pallas_call(kernel, out_shape=outs, compiler_params=PARAMS)(*args)
-
-
 IMAGE = shape(5, 64, 128)
-TRACES = shape(6, 80, 128)
 EDGE = shape(120, 128)
 SLOTS = shape(160, 128)
 MESSAGE = shape(4, 160, 128)
@@ -379,68 +377,61 @@
 RIM_HOTS = shape(6, 128, 128, kind=BF16)
 
 
-def exchange(edge, message):
-    ends = [(4 * c + 3, 4 * c + 4) for c in range(lax.axis_size("curve") - 1)]
-    message = lax.all_to_all(message, "group", split_axis=0, concat_axis=0, tiled=True)
-    edge = lax.ppermute(edge, AXES, ends + [(j, i) for i, j in ends])
-    return edge, message
-
-
 VMEM = pl.BlockSpec(memory_space=pltpu.VMEM)
 HBM = pl.BlockSpec(memory_space=pltpu.HBM)
-MESSAGE_SCRATCH = [pltpu.VMEM(MESSAGE.shape, F32)]
-TWO_COPIES = pltpu.SemaphoreType.DMA((2,))
-
-
-def in_hbm(*args):
-    return [pltpu.with_memory_space_constraint(x, pltpu.HBM) for x in args]
+TRACES = pltpu.VMEM((6, 80, 128), F32)
+SEND_SCRATCH = [
+    TRACES,
+    TRACES,
+    pltpu.VMEM((4, 40, 128), F32),
+    pltpu.VMEM((2, 120, 128), F32),
+    pltpu.SemaphoreType.DMA((3,)),
+]
+
+
+def exchange(edge, message):
+    count = lax.axis_size(AXES)
+    pairs = [[0, 1], [count - 2, count - 1]]
+    pairs += [[d + i, d + j] for d in range(0, count - 4, 4) for i, j in ((3, 4), (2, 5))]
+    message = lax.all_to_all(message, "group", split_axis=0, concat_axis=0, tiled=True)
+    edge = lax.all_gather(edge, AXES, axis_index_groups=pairs, axis=0, tiled=True)
+    return edge, message
 
 
 def local(tangent, jacobian, viscosity, neighbours, send_table, recv_table):
     volume_table, inter_table, project_table = (jnp.asarray(t) for t in operator_tables())
-    jacobian = jnp.transpose(jacobian, (1, 2, 0, 3))
-    inputs = (tangent, jacobian, send_table, recv_table, inter_table)
-    g, h, edge, message, slots, tangent, jacobian, recv_table, inter_table = pl.pallas_call(
+    inputs = (
+        tangent, jnp.transpose(jacobian, (1, 2, 0, 3)), send_table, recv_table, inter_table,
+        viscosity, neighbours, volume_table, project_table,
+    )
+    kept = [inputs[i] for i in (1, 3, 4, 5, 6, 7, 8)]
+    edge, message, slots, base, loc, hots, *kept = pl.pallas_call(
         first_kernel,
-        out_shape=(TRACES, TRACES, EDGE, MESSAGE, SLOT_HOTS)
-        + tuple(pltpu.VMEM(inputs[i].shape, inputs[i].dtype) for i in (0, 1, 3, 4)),
-        in_specs=[HBM] * 5,
-        out_specs=(VMEM, VMEM, VMEM, HBM) + (VMEM,) * 5,
-        scratch_shapes=[pltpu.VMEM(send_table.shape, send_table.dtype)]
-        + MESSAGE_SCRATCH
-        + [pltpu.SemaphoreType.DMA((5,)), TWO_COPIES],
+        out_shape=(EDGE, MESSAGE, SLOT_HOTS, IMAGE, SLOTS, RIM_HOTS)
+        + tuple(pltpu.VMEM(x.shape, x.dtype) for x in kept),
+        in_specs=[HBM] * 9,
+        out_specs=(VMEM, HBM) + (VMEM,) * 11,
+        scratch_shapes=[
+            pltpu.VMEM(tangent.shape, F32), pltpu.VMEM(send_table.shape, send_table.dtype)
+        ]
+        + SEND_SCRATCH
+        + [pltpu.SemaphoreType.DMA((9,))],
         compiler_params=PARAMS,
-    )(*in_hbm(*inputs))
+    )(*(pltpu.with_memory_space_constraint(x, pltpu.HBM) for x in inputs))
     edge, message = exchange(edge, message)
-    inputs = (viscosity, neighbours, volume_table, project_table)
-    base, loc, hots, viscosity, neighbours, volume_table, project_table = pl.pallas_call(
-        first_local,
-        out_shape=(IMAGE, SLOTS, RIM_HOTS) + tuple(pltpu.VMEM(x.shape, x.dtype) for x in inputs),
-        in_specs=[VMEM] * 7 + [HBM] * 4,
-        out_specs=(VMEM,) * 7,
-        scratch_shapes=[pltpu.SemaphoreType.DMA((4,))],
+    first, edge, message, base, loc = pl.pallas_call(
+        middle_kernel,
+        out_shape=(IMAGE, EDGE, MESSAGE, IMAGE, SLOTS),
+        in_specs=[VMEM] * 13,
+        out_specs=(HBM, VMEM, HBM, VMEM, VMEM),
+        scratch_shapes=[pltpu.VMEM(IMAGE.shape, F32)] + SEND_SCRATCH + [pltpu.SemaphoreType.DMA],
         compiler_params=PARAMS,
-    )(tangent, jacobian, g, h, slots, recv_table, inter_table, *in_hbm(*inputs))
-    base = call(group_part, IMAGE, base, loc, message, hots, slots, recv_table, project_table)
-    image, g, h, edge, message = pl.pallas_call(
-        middle_kernel,
-        out_shape=(pltpu.VMEM(IMAGE.shape, F32), TRACES, TRACES, EDGE, MESSAGE),
-        in_specs=[VMEM] * 7,
-        out_specs=(VMEM, VMEM, VMEM, VMEM, HBM),
-        scratch_shapes=MESSAGE_SCRATCH + [TWO_COPIES],
-        compiler_params=PARAMS,
-    )(base, edge, hots, slots, recv_table, jacobian, inter_table)
+    )(base, loc, message, edge, hots, slots, *kept)
     edge, message = exchange(edge, message)
-    base, loc, first = pl.pallas_call(
-        second_local,
-        out_shape=(IMAGE, SLOTS, IMAGE),
-        in_specs=[VMEM] * 10,
-        out_specs=(VMEM, VMEM, HBM),
-        scratch_shapes=[pltpu.SemaphoreType.DMA],
-        compiler_params=PARAMS,
-    )(image, jacobian, viscosity, neighbours, g, h, slots, recv_table, volume_table, inter_table)
-    base = call(group_part, IMAGE, base, loc, message, hots, slots, recv_table, project_table)
-    second = call(edge_part, IMAGE, base, edge, hots)
+    recv_table, project_table = kept[1], kept[6]
+    second = pl.pallas_call(
+        last_kernel, out_shape=IMAGE, in_specs=[VMEM] * 8, out_specs=VMEM, compiler_params=PARAMS
+    )(base, loc, message, edge, hots, slots, recv_table, project_table)
     return first, second
 
 

time: 45.7 us -> 44.9 us (0.982)
  blocking collectives: 0 us -> 30.1 us
  starting transfers between devices: 36.3 us -> 7.77 us
  Pallas kernels: 7.78 us -> 6.08 us
  waiting for transfers between devices: 0.56 us -> 0.01 us
    all_gather x0 -> x2, blocking collectives: none -> 30.1 us  [exchange(): lax.all_gather(edge, AXES, axis_index_groups=pairs, axis=0, tiled=True)]
    ppermute x2 -> x0, starting transfers between devices: 28.6 us -> none  [exchange(): edge = lax.ppermute(edge, AXES, ends + [(j, i) for i, j in ends])]
    pallas_call x7 -> x3, Pallas kernels: 7.78 us -> 6.08 us  [the longest x1 2.38 us: local(): pl.pallas_call(middle_kernel, out_shape=(IMAGE, EDGE, MESSAGE, IMAGE, SLO...]
    ppermute x2 -> x0, waiting for transfers between devices: 0.55 us -> none  [exchange(): edge = lax.ppermute(edge, AXES, ends + [(j, i) for i, j in ends])]
  transfers between devices with their start and end apart: 4 -> 2, of which waited for: 1 -> 0; matrix products, arithmetic and copies ran while one was open for 0% -> 0% of each run, Pallas kernels for 7% -> 0%
where the time goes in v5:
time: 44.9 us; the launch traced here: 44.6 us
  blocking collectives  30.1 us (67%)
  starting transfers between devices  7.77 us (17%)
  Pallas kernels  6.08 us (14%)
  between operations  0.66 us (1%)
    all_gather x2, blocking collectives, exchange(): lax.all_gather(edge, AXES, axis_index_groups=pairs, axis=0, tiled=True)  30.1 us
    all_to_all x2, starting transfers between devices, exchange(): lax.all_to_all(message, 'group', split_axis=0, concat_axis=0, tiled=True)  7.77 us
    pallas_call x1, Pallas kernels, local(): pl.pallas_call(middle_kernel, out_shape=(IMAGE, EDGE, MESSAGE, IMAGE, SLO...  2.38 us
    pallas_call x1, Pallas kernels, local(): pl.pallas_call(first_kernel, out_shape=(EDGE, MESSAGE, SLOT_HOTS, IMAGE,...  2.27 us
    pallas_call x1, Pallas kernels, local(): pl.pallas_call(last_kernel, out_shape=IMAGE, in_specs=[VMEM] * 8, out_spe...  1.42 us
  transfers between devices with their start and end apart: 2, of which 0 were waited for; matrix products, arithmetic and copies ran while one was open for 0% of the time, Pallas kernels for 0%

profile of v5, /device:TPU:24, one launch (start us, length us, event | category | flops | bytes accessed | tf_op | source)
XLA Modules:
  0.0 44.6 jit_solution(6522892688042532027)
XLA Ops:
  0.6 2.3 %shard_map.104 = (f32[120,128]{1,0:T(8,128)S(1)}, f32[4,160,128]{2,1,0:T(8,128)}, bf16[768,256]{1,0:T(8,128)(2,1)S(1)}, f32[5,64,128]{2,1,0:T(8,128)S(1)}, f32[1...) custom-call(f32[5,64,128]{2,1,0:T(8,128)} %v_hbm.1, ...), custom_call_target="tpu_custom_call" | custom-call | tf_op jit(solution)/shard_map/pallas_call | solution.py:408
  2.9 4.3 %all-to-all-start = ((f32[4,160,128]{2,1,0:T(8,128)}), f32[4,160,128]{2,1,0:T(8,128)S(1)}, u32[]{:S(2)}, u32[]{:S(2)}) async-start(f32[4,160,128]{2,1,0:T(8,128)} %get-tuple-element.22), calls=%async_computation | async-start | bytes 655360 | tf_op jit(solution)/shard_map/all_to_all | solution.py:396
  7.2 21.0 %all_gather.6.edge_ref = f32[240,128]{1,0:T(8,128)S(1)} all-gather(f32[120,128]{1,0:T(8,128)S(1)} %get-tuple-element.23), channel_id=1, replica_groups={{0,1},{1022,1023},{3,4},{2,5},{7,8},{6,9},{11,12},{10,13},{15,16},{14,1..., dimensions={0}, use_global_device_ids=true | all-gather | bytes 184320 | tf_op jit(solution)/shard_map/all_gather | solution.py:397
  28.3 0.0 all-to-all-done.m_ref
  28.3 2.4 %shard_map.105 = (f32[5,64,128]{2,1,0:T(8,128)}, f32[120,128]{1,0:T(8,128)S(1)}, f32[4,160,128]{2,1,0:T(8,128)}, f32[5,64,128]{2,1,0:T(8,128)S(1)}, f32[160,128]{1,0:T(8,128)S(1)}) custom-call(f32[5,64,128]{2,1,0:T(8,128)S(1)} %get-tuple-element.20.base_ref, f32[160,128]{1,0:T(8,128)S(1)} %get-tuple-element.21.loc_ref, ...), custom_call_target="tpu_custom_call" | custom-call | tf_op jit(solution)/shard_map/pallas_call | solution.py:422
  30.7 3.5 %all-to-all-start.1 = ((f32[4,160,128]{2,1,0:T(8,128)}), f32[4,160,128]{2,1,0:T(8,128)S(1)}, u32[]{:S(2)}, u32[]{:S(2)}) async-start(f32[4,160,128]{2,1,0:T(8,128)} %get-tuple-element.36), calls=%async_computation.1 | async-start | bytes 655360 | tf_op jit(solution)/shard_map/all_to_all | solution.py:396
  34.1 9.0 %all_gather.7.edge_ref = f32[240,128]{1,0:T(8,128)S(1)} all-gather(f32[120,128]{1,0:T(8,128)S(1)} %get-tuple-element.37), channel_id=1, replica_groups={{0,1},{1022,1023},{3,4},{2,5},{7,8},{6,9},{11,12},{10,13},{15,16},{14,1..., dimensions={0}, use_global_device_ids=true | all-gather | bytes 184320 | tf_op jit(solution)/shard_map/all_gather | solution.py:397
  43.2 0.0 all-to-all-done.1.m_ref
  43.2 1.4 %shard_map.106 = f32[5,64,128]{2,1,0:T(8,128)} custom-call(f32[5,64,128]{2,1,0:T(8,128)S(1)} %get-tuple-element.34.base_ref, f32[160,128]{1,0:T(8,128)S(1)} %get-tuple-element.35.loc_ref, f32[4,160,128]{2,1,0:T(8,128)S(1)} %all-to-all-done.1.m_ref, f32[240,128]{1,0:T(8,128)S(1)} %all_gather.7.edge_ref, bf16[6,128,128]{2,1,0:T(8,128)(2,1)S(1)} %get-tuple-element.24.hot_ref, ...), custom_call_target="tpu_custom_call" | custom-call | tf_op jit(solution)/shard_map/pallas_call | solution.py:432
Async XLA Ops:
  2.9 25.4 %all-to-all-start = ((f32[4,160,128]{2,1,0:T(8,128)}), f32[4,160,128]{2,1,0:T(8,128)S(1)}, u32[]{:S(2)}, u32[]{:S(2)}) async-start(f32[4,160,128]{2,1,0:T(8,128)} %get-tuple-element.22), calls=%async_computation | async-start | bytes 655360 | tf_op jit(solution)/shard_map/all_to_all | solution.py:396
  30.7 12.5 %all-to-all-start.1 = ((f32[4,160,128]{2,1,0:T(8,128)}), f32[4,160,128]{2,1,0:T(8,128)S(1)}, u32[]{:S(2)}, u32[]{:S(2)}) async-start(f32[4,160,128]{2,1,0:T(8,128)} %get-tuple-element.36), calls=%async_computation.1 | async-start | bytes 655360 | tf_op jit(solution)/shard_map/all_to_all | solution.py:396

commit v6 on v5

--- a/solution.py
+++ b/solution.py
@@ -341,25 +341,28 @@
 def middle_kernel(
     base_ref, loc_ref, m_ref, edge_ref, hot_ref, slot_ref,
     j_ref, recv_ref, it_ref, visc_ref, nb_ref, vt_ref, pt_ref,
-    v_hbm, edge2_ref, m_hbm, base2_ref, loc2_ref,
-    v_ref, g_ref, h_ref, slots_ref, rims_ref, m_sems, sem,
+    v_ref, edge2_ref, m_hbm, base2_ref, loc2_ref,
+    g_ref, h_ref, slots_ref, rims_ref, m_sems,
 ):
     group_part(base_ref, loc_ref, m_ref, hot_ref, slot_ref, recv_ref, pt_ref, v_ref)
     edge_part(edge_ref, hot_ref, v_ref)
     g = trace_part(v_ref, j_ref, g_ref, h_ref)
     sent = send_part(g, slot_ref[...], recv_ref, it_ref, edge2_ref, slots_ref, rims_ref, m_hbm, m_sems)
-    image = pltpu.make_async_copy(v_ref, v_hbm, sem)
-    image.start()
     slot_terms(h_ref, slot_ref, recv_ref, it_ref, loc2_ref)
     local_part(v_ref, j_ref, visc_ref, nb_ref, g_ref, h_ref, vt_ref, base2_ref)
     for copy in sent:
         copy.wait()
-    image.wait()
-
-
-def last_kernel(base_ref, loc_ref, m_ref, edge_ref, hot_ref, slot_ref, recv_ref, pt_ref, o_ref):
+
+
+def last_kernel(
+    v_ref, base_ref, loc_ref, m_ref, edge_ref, hot_ref, slot_ref, recv_ref, pt_ref,
+    v_hbm, o_ref, sem,
+):
+    image = pltpu.make_async_copy(v_ref, v_hbm, sem)
+    image.start()
     group_part(base_ref, loc_ref, m_ref, hot_ref, slot_ref, recv_ref, pt_ref, o_ref)
     edge_part(edge_ref, hot_ref, o_ref)
+    image.wait()
 
 
 def shape(*dims, kind=F32):
@@ -419,19 +422,24 @@
         compiler_params=PARAMS,
     )(*(pltpu.with_memory_space_constraint(x, pltpu.HBM) for x in inputs))
     edge, message = exchange(edge, message)
-    first, edge, message, base, loc = pl.pallas_call(
+    image, edge, message, base, loc = pl.pallas_call(
         middle_kernel,
-        out_shape=(IMAGE, EDGE, MESSAGE, IMAGE, SLOTS),
+        out_shape=(pltpu.VMEM(IMAGE.shape, F32), EDGE, MESSAGE, IMAGE, SLOTS),
         in_specs=[VMEM] * 13,
-        out_specs=(HBM, VMEM, HBM, VMEM, VMEM),
-        scratch_shapes=[pltpu.VMEM(IMAGE.shape, F32)] + SEND_SCRATCH + [pltpu.SemaphoreType.DMA],
+        out_specs=(VMEM, VMEM, HBM, VMEM, VMEM),
+        scratch_shapes=SEND_SCRATCH,
         compiler_params=PARAMS,
     )(base, loc, message, edge, hots, slots, *kept)
     edge, message = exchange(edge, message)
     recv_table, project_table = kept[1], kept[6]
-    second = pl.pallas_call(
-        last_kernel, out_shape=IMAGE, in_specs=[VMEM] * 8, out_specs=VMEM, compiler_params=PARAMS
-    )(base, loc, message, edge, hots, slots, recv_table, project_table)
+    first, second = pl.pallas_call(
+        last_kernel,
+        out_shape=(IMAGE, IMAGE),
+        in_specs=[VMEM] * 9,
+        out_specs=(HBM, VMEM),
+        scratch_shapes=[pltpu.SemaphoreType.DMA],
+        compiler_params=PARAMS,
+    )(image, base, loc, message, edge, hots, slots, recv_table, project_table)
     return first, second
 
 

time: 44.9 us -> 44.9 us (level)
  no operation moved by 1% of the time
where the time goes in v6:
time: 44.9 us; the launch traced here: 44.6 us
  blocking collectives  30.1 us (67%)
  starting transfers between devices  7.77 us (17%)
  Pallas kernels  6.08 us (14%)
  between operations  0.66 us (1%)
    all_gather x2, blocking collectives, exchange(): lax.all_gather(edge, AXES, axis_index_groups=pairs, axis=0, tiled=True)  30.1 us
    all_to_all x2, starting transfers between devices, exchange(): lax.all_to_all(message, 'group', split_axis=0, concat_axis=0, tiled=True)  7.77 us
    pallas_call x1, Pallas kernels, local(): pl.pallas_call(middle_kernel, out_shape=(pltpu.VMEM(IMAGE.shape, F32), ED...  2.37 us
    pallas_call x1, Pallas kernels, local(): pl.pallas_call(first_kernel, out_shape=(EDGE, MESSAGE, SLOT_HOTS, IMAGE,...  2.27 us
    pallas_call x1, Pallas kernels, local(): pl.pallas_call(last_kernel, out_shape=(IMAGE, IMAGE), in_specs=[VMEM] * 9...  1.43 us
  transfers between devices with their start and end apart: 2, of which 0 were waited for; matrix products, arithmetic and copies ran while one was open for 0% of the time, Pallas kernels for 0%

profile of v6, /device:TPU:24, one launch (start us, length us, event | category | flops | bytes accessed | tf_op | source)
XLA Modules:
  0.0 44.6 jit_solution(17390171962497023798)
XLA Ops:
  0.6 2.3 %shard_map.104 = (f32[120,128]{1,0:T(8,128)S(1)}, f32[4,160,128]{2,1,0:T(8,128)}, bf16[768,256]{1,0:T(8,128)(2,1)S(1)}, f32[5,64,128]{2,1,0:T(8,128)S(1)}, f32[1...) custom-call(f32[5,64,128]{2,1,0:T(8,128)} %v_hbm.1, ...), custom_call_target="tpu_custom_call" | custom-call | tf_op jit(solution)/shard_map/pallas_call | solution.py:411
  2.9 4.3 %all-to-all-start = ((f32[4,160,128]{2,1,0:T(8,128)}), f32[4,160,128]{2,1,0:T(8,128)S(1)}, u32[]{:S(2)}, u32[]{:S(2)}) async-start(f32[4,160,128]{2,1,0:T(8,128)} %get-tuple-element.22), calls=%async_computation | async-start | bytes 655360 | tf_op jit(solution)/shard_map/all_to_all | solution.py:399
  7.2 21.0 %all_gather.6.edge_ref = f32[240,128]{1,0:T(8,128)S(1)} all-gather(f32[120,128]{1,0:T(8,128)S(1)} %get-tuple-element.23), channel_id=1, replica_groups={{0,1},{1022,1023},{3,4},{2,5},{7,8},{6,9},{11,12},{10,13},{15,16},{14,1..., dimensions={0}, use_global_device_ids=true | all-gather | bytes 184320 | tf_op jit(solution)/shard_map/all_gather | solution.py:400
  28.3 0.0 all-to-all-done.m_ref
  28.3 2.4 %shard_map.105 = (f32[5,64,128]{2,1,0:T(8,128)S(1)}, f32[120,128]{1,0:T(8,128)S(1)}, f32[4,160,128]{2,1,0:T(8,128)}, f32[5,64,128]{2,1,0:T(8,128)S(1)}, f32[160,128]{1,0:T(8,128)S(1)}) custom-call(f32[5,64,128]{2,1,0:T(8,128)S(1)} %get-tuple-element.20.base_ref, f32[160,128]{1,0:T(8,128)S(1)} %get-tuple-element.21.loc_ref, ...), custom_call_target="tpu_custom_call" | custom-call | tf_op jit(solution)/shard_map/pallas_call | solution.py:425
  30.6 3.5 %all-to-all-start.1 = ((f32[4,160,128]{2,1,0:T(8,128)}), f32[4,160,128]{2,1,0:T(8,128)S(1)}, u32[]{:S(2)}, u32[]{:S(2)}) async-start(f32[4,160,128]{2,1,0:T(8,128)} %get-tuple-element.36), calls=%async_computation.1 | async-start | bytes 655360 | tf_op jit(solution)/shard_map/all_to_all | solution.py:399
  34.1 9.0 %all_gather.7.edge_ref = f32[240,128]{1,0:T(8,128)S(1)} all-gather(f32[120,128]{1,0:T(8,128)S(1)} %get-tuple-element.37), channel_id=1, replica_groups={{0,1},{1022,1023},{3,4},{2,5},{7,8},{6,9},{11,12},{10,13},{15,16},{14,1..., dimensions={0}, use_global_device_ids=true | all-gather | bytes 184320 | tf_op jit(solution)/shard_map/all_gather | solution.py:400
  43.1 0.0 all-to-all-done.1.m_ref
  43.1 1.4 %shard_map.106 = (f32[5,64,128]{2,1,0:T(8,128)}, f32[5,64,128]{2,1,0:T(8,128)}) custom-call(f32[5,64,128]{2,1,0:T(8,128)S(1)} %get-tuple-element.33.v_ref, f32[5,64,128]{2,1,0:T(8,128)S(1)} %get-tuple-element.34.base_ref, f32[160,128]{1,0:T(8,128)S(1)} %get-tuple-element.35.loc_ref, f32[4,160,128]{2,1,0:T(8,128)S(1)} %all-to-all-done.1.m_ref, ...), custom_call_target="tpu_custom_call" | custom-call | tf_op jit(solution)/shard_map/pallas_call | solution.py:435
Async XLA Ops:
  2.9 25.4 %all-to-all-start = ((f32[4,160,128]{2,1,0:T(8,128)}), f32[4,160,128]{2,1,0:T(8,128)S(1)}, u32[]{:S(2)}, u32[]{:S(2)}) async-start(f32[4,160,128]{2,1,0:T(8,128)} %get-tuple-element.22), calls=%async_computation | async-start | bytes 655360 | tf_op jit(solution)/shard_map/all_to_all | solution.py:399
  30.6 12.5 %all-to-all-start.1 = ((f32[4,160,128]{2,1,0:T(8,128)}), f32[4,160,128]{2,1,0:T(8,128)S(1)}, u32[]{:S(2)}, u32[]{:S(2)}) async-start(f32[4,160,128]{2,1,0:T(8,128)} %get-tuple-element.36), calls=%async_computation.1 | async-start | bytes 655360 | tf_op jit(solution)/shard_map/all_to_all | solution.py:399
